TPU v7x, 32 devices: a whole 2x2x4 slice. The times are simulated.
32 devices in a mesh: ao: 4 (over z), fit: 8 (over y, x, core).
Axes of the slice: x: 2, y: 2, z: 4, core: 2. Of those that a mesh axis runs over, the one named last changes fastest.
Arguments:
- coefficients: bfloat16 [512, 128], P('ao'), may hold values from -2 to 2
- three_center: bfloat16 [32, 512, 4096], P('fit', 'ao'), may hold values from -0.09375 to 0.09375
- pair_blocks: int32 [4, 32], P('ao'), may hold values from 0 to 3
- pair_count: int32 [4], P('ao'), may hold values from 1 to 32, as said below
Outputs:
- exchange: float32 [512, 512], P('ao', 'fit')
Inputs may be any that keep to these rules, and one draw needn't show every extreme that they name: Row block m uses its first pair_count[m] slots; some row block has all 32 live in every draw.
All inputs are finite; a program needn't handle non-finite values.
Results may differ from a plain program's by a relative error of at most 0.0012.
Values may be sent and summed in bfloat16 or wider, within the bound.
No kernel may reach another device: no remote copies, remote signals or barrier semaphores. Data moves between devices by JAX's collectives and lax.ppermute only.
A program may use at most 64 MiB of HBM per device.

v0:
```python
import jax
import jax.numpy as jnp
from jax import lax
from jax.sharding import PartitionSpec as P


def per_device(coefficients, three_center, pair_blocks, pair_count):
    fit_dev = three_center.shape[0]
    block = three_center.shape[1]
    pairs = pair_blocks.shape[1]
    orbitals = coefficients.shape[1]
    every = lax.all_gather(coefficients, "ao", axis=0, tiled=True)
    chosen = every.reshape(-1, block, orbitals)[pair_blocks[0]]
    live = (jnp.arange(pairs, dtype=jnp.int32) < pair_count[0])[:, None, None]
    chosen = jnp.where(live, chosen, jnp.zeros_like(chosen)).reshape(pairs * block, orbitals)
    half = jnp.dot(
        three_center.reshape(fit_dev * block, pairs * block),
        chosen,
        preferred_element_type=jnp.float32,
    )
    half = half.astype(jnp.bfloat16).reshape(fit_dev, block, orbitals)
    terms = jnp.einsum(
        "fmi,fni->mn",
        half,
        lax.all_gather(half, "ao", axis=1, tiled=True),
        preferred_element_type=jnp.float32,
    )
    return lax.psum_scatter(terms, "fit", scatter_dimension=1, tiled=True)


def solution(mesh):
    return jax.shard_map(
        per_device,
        mesh=mesh,
        in_specs=(P("ao", None), P("fit", "ao", None), P("ao", None), P("ao")),
        out_specs=P("ao", "fit"),
        check_vma=False,
    )
```

profile of v0, /device:TPU:0, one launch (start us, length us, event | category | flops | bytes accessed | tf_op | source)
XLA Modules:
  0.0 85.9 jit_solution(7206830381649446189)
XLA Ops:
  6.5 0.0 reduce-scatter.2.cloned.1.call-start
  6.5 15.3 %all_gather.6 = bf16[512,128]{1,0:T(8,128)(2,1)S(1)} all-gather(bf16[128,128]{1,0:T(8,128)(2,1)} %param.4), channel_id=1, replica_groups=mesh['ao'=4,'fit'=8] {'ao'}, dimensions={0}, use_global_device_ids=true | all-gather | bytes 163840 | tf_op jit(solution)/shard_map/all_gather | solution.py:12
  21.8 0.7 fusion.1
  23.1 0.7 gather_fusion
  23.9 0.1 broadcast_select_fusion
  24.0 3.7 %fusion = bf16[512,128]{0,1:T(8,128)(2,1)S(1)} fusion(bf16[4096,128]{1,0:T(8,128)(2,1)S(1)} %bitcast.20, bf16[512,4096]{1,0:T(8,128)(2,1)} %bitcast.19), kind=kOutput, calls=%fused_computation.3 | convolution fusion | flops 536936448 | bytes 5373952 | tf_op jit(solution)/shard_map/dot_general | solution.py:16
  27.8 0.1 copy.7
  27.9 16.0 %all_gather.7 = bf16[4,512,128]{2,1,0:T(8,128)(2,1)S(1)} all-gather(bf16[4,128,128]{2,1,0:T(8,128)(2,1)S(1)} %bitcast.21), channel_id=1, replica_groups=mesh['ao'=4,'fit'=8] {'ao'}, dimensions={1}, use_global_device_ids=true | all-gather | bytes 655360 | tf_op jit(solution)/shard_map/all_gather | solution.py:25
  43.9 1.0 %convolution_bitcast_fusion = f32[128,512]{0,1:T(8,128)} fusion(bf16[4,128,128]{2,1,0:T(8,128)(2,1)S(1)} %bitcast.22, bf16[4,512,128]{2,1,0:T(8,128)(2,1)S(1)} %all_gather.7), kind=kOutput, calls=%fused_computation.1 | convolution fusion | flops 67108864 | bytes 917504 | tf_op jit(solution)/shard_map/fmi,fni->mn/dot_general | solution.py:22
  44.9 0.0 reduce-scatter.2.cloned.1.call-update
  44.9 34.2 %reduce-scatter.2.cloned.1.call-done = f32[128,64]{0,1:T(8,128)} async-done(((f32[128,512]{0,1:T(8,128)}), f32[128,64]{0,1:T(8,128)}) %reduce-scatter.2.cloned.1.call-update) | async-done | bytes 32784 | tf_op jit(solution)/shard_map/reduce_scatter | solution.py:28
  (2 shorter events, 0.0 us)
Async XLA Ops:
  6.5 72.5 %reduce-scatter.2.cloned.1.call-start = ((), (), s32[]{:S(2)}) async-start(), calls=%async_computation.1 | async-start | bytes 294912 | tf_op jit(solution)/shard_map/reduce_scatter | solution.py:28
Sparse Core Ops, SparseCore 0:
  45.0 34.0 reduce-scatter.1
where the time goes:
time: 86.1 us; the launch traced here: 85.9 us
  waiting for transfers between devices  34.2 us (40%)
  blocking collectives  31.2 us (36%)
  between operations  14.1 us (16%)
  matrix products  4.71 us (5%)
  local copies, waits for them, and re-layouts  0.87 us (1%)
    reduce_scatter x1, waiting for transfers between devices, per_device(): return lax.psum_scatter(terms, 'fit', scatter_dimension=1, tiled=True)  34.2 us
    all_gather x1, blocking collectives, per_device(): lax.all_gather(half, 'ao', axis=1, tiled=True)  16 us
    all_gather x1, blocking collectives, per_device(): every = lax.all_gather(coefficients, 'ao', axis=0, tiled=True)  15.3 us
    dot_general x1, matrix products, per_device(): jnp.dot(three_center.reshape(fit_dev * block, pairs * block), chosen, pre...  3.71 us
  transfers between devices with their start and end apart: 1, of which 1 were waited for; matrix products, arithmetic and copies ran while one was open for 0% of the time, Pallas kernels for 0%

commit v1 on v0

--- a/solution.py
+++ b/solution.py
@@ -1,10 +1,17 @@
+import functools
+
 import jax
 import jax.numpy as jnp
 from jax import lax
+from jax.experimental import pallas as pl
+from jax.experimental.pallas import tpu as pltpu
 from jax.sharding import PartitionSpec as P
 
+VMEM = pl.BlockSpec(memory_space=pltpu.VMEM)
+SMEM = pl.BlockSpec(memory_space=pltpu.SMEM)
 
-def per_device(coefficients, three_center, pair_blocks, pair_count):
+
+def gathered_form(coefficients, three_center, pair_blocks, pair_count):
     fit_dev = three_center.shape[0]
     block = three_center.shape[1]
     pairs = pair_blocks.shape[1]
@@ -28,7 +35,125 @@
     return lax.psum_scatter(terms, "fit", scatter_dimension=1, tiled=True)
 
 
+def slot_sums(blocks, pairs, width, pair_ref, count_ref, x_ref, sums_ref, acc):
+    z = lax.axis_index("ao")
+    acc[...] = jnp.zeros_like(acc)
+
+    def add(p, carry):
+        place = pair_ref[0, p] ^ z
+        acc[place] += x_ref[0, :, pl.ds(pl.multiple_of(p * width, width), width)].astype(jnp.float32)
+        return carry
+
+    lax.fori_loop(0, jnp.minimum(count_ref[0], pairs), add, 0)
+    for b in range(blocks):
+        whole = acc[b]
+        high = whole.astype(jnp.bfloat16)
+        sums_ref[:, b * width : (b + 1) * width] = high
+        sums_ref[:, (blocks + b) * width : (blocks + b + 1) * width] = (whole - high.astype(jnp.float32)).astype(jnp.bfloat16)
+
+
+def transform(blocks, sums_ref, *refs):
+    half_ref = refs[-1]
+    coefficients = jnp.concatenate([ref[...] for ref in refs[:-1]] * 2, axis=0)
+    half = jnp.dot(sums_ref[...], coefficients, preferred_element_type=jnp.float32)
+    half_ref[...] = half.astype(jnp.bfloat16).reshape(half_ref.shape)
+
+
+def products(blocks, fits, *refs):
+    halves, keep_ref, send_ref, whole = refs[:blocks], refs[blocks], refs[blocks + 1], refs[blocks + 2]
+    z, f = lax.axis_index("ao"), lax.axis_index("fit")
+    q, core = f // 2, f % 2
+    columns = keep_ref.shape[1]
+    for k in range(blocks):
+        total = None
+        for p in range(fits):
+            term = lax.dot_general(
+                halves[k][p], halves[0][p], (((1,), (1,)), ((), ())), preferred_element_type=jnp.float32
+            )
+            total = term if total is None else total + term
+        whole[k] = total
+    for k in range(blocks):
+        place = z ^ q ^ k
+        keep_ref[place] = whole[k, pl.ds(pl.multiple_of(core * columns, columns), columns), :]
+        send_ref[place] = whole[k, pl.ds(pl.multiple_of((1 - core) * columns, columns), columns), :]
+
+
+def finish(own_ref, *refs):
+    out_ref = refs[-1]
+    total = own_ref[...]
+    for ref in refs[:-1]:
+        total = total + ref[...]
+    out_ref[...] = total.T
+
+
+def permuted_form(blocks, coefficients, three_center, pair_blocks, pair_count):
+    fits, block, wide = three_center.shape
+    pairs = pair_blocks.shape[1]
+    orbitals = coefficients.shape[1]
+    columns = block // 2
+    chips = range(1, blocks)
+
+    def over_ao(x):
+        return [lax.ppermute(x, "ao", [(i, i ^ k) for i in range(blocks)]) for k in chips]
+
+    def over_fit(x, k):
+        return lax.ppermute(x, "fit", [(i, i ^ k) for i in range(2 * blocks)])
+
+    coefs = [coefficients] + over_ao(coefficients)
+    sums = pl.pallas_call(
+        functools.partial(slot_sums, blocks, pairs, block),
+        grid=(fits,),
+        out_shape=jax.ShapeDtypeStruct((fits * block, 2 * blocks * block), jnp.bfloat16),
+        in_specs=[SMEM, SMEM, pl.BlockSpec((1, block, wide), lambda i: (i, 0, 0))],
+        out_specs=pl.BlockSpec((block, 2 * blocks * block), lambda i: (i, 0)),
+        scratch_shapes=[pltpu.VMEM((blocks, block, block), jnp.float32)],
+        name="slot_sums",
+    )(pair_blocks, pair_count, three_center)
+    half = pl.pallas_call(
+        functools.partial(transform, blocks),
+        out_shape=jax.ShapeDtypeStruct((fits, block, orbitals), jnp.bfloat16),
+        in_specs=[VMEM] * (blocks + 1),
+        out_specs=VMEM,
+        name="transform",
+    )(sums, *coefs)
+    halves = [half] + over_ao(half)
+    piece = jax.ShapeDtypeStruct((blocks, columns, block), jnp.float32)
+    keep, send = pl.pallas_call(
+        functools.partial(products, blocks, fits),
+        out_shape=(piece, piece),
+        in_specs=[VMEM] * blocks,
+        out_specs=(VMEM, VMEM),
+        scratch_shapes=[pltpu.VMEM((blocks, block, block), jnp.float32)],
+        name="products",
+    )(*halves)
+    chip = keep + over_fit(send, 1)
+    parts = [chip[0]] + [over_fit(chip[k], 2 * k) for k in chips]
+    return pl.pallas_call(
+        finish,
+        out_shape=jax.ShapeDtypeStruct((block, columns), jnp.float32),
+        in_specs=[VMEM] * blocks,
+        out_specs=VMEM,
+        name="finish",
+    )(*parts)
+
+
 def solution(mesh):
+    blocks, fit = mesh.shape["ao"], mesh.shape["fit"]
+
+    def per_device(coefficients, three_center, pair_blocks, pair_count):
+        block = three_center.shape[1]
+        fast = (
+            fit == 2 * blocks
+            and blocks & (blocks - 1) == 0
+            and 1 < blocks <= 4
+            and block % 128 == 0
+            and coefficients.shape[1] % 128 == 0
+            and coefficients.shape[0] == block
+            and pair_blocks.shape[0] == 1
+        )
+        form = functools.partial(permuted_form, blocks) if fast else gathered_form
+        return form(coefficients, three_center, pair_blocks, pair_count)
+
     return jax.shard_map(
         per_device,
         mesh=mesh,

time: 86.1 us -> 45.9 us (0.53)
  blocking collectives: 31.2 us -> 0 us
  waiting for transfers between devices: 34.2 us -> 15 us
  starting transfers between devices: 0.01 us -> 13.5 us
  between operations: 14.1 us -> 0.69 us
  Pallas kernels: 0 us -> 10.8 us
  matrix products: 4.71 us -> 0 us
  local copies, waits for them, and re-layouts: 0.87 us -> 4.71 us
    reduce_scatter x1 -> x0, waiting for transfers between devices: 34.2 us -> none  [per_device(): return lax.psum_scatter(terms, 'fit', scatter_dimension=1, tiled=True)]
    all_gather x2 -> x0, blocking collectives: 31.2 us -> none  [the longest x1 16 us: per_device(): lax.all_gather(half, 'ao', axis=1, tiled=True)]
    ppermute x0 -> x10, waiting for transfers between devices: none -> 15 us  [the longest x6 10.1 us: over_ao(): lax.ppermute(x, 'ao', [(i, i ^ k) for i in range(blocks)])]
    ppermute x0 -> x10, starting transfers between devices: none -> 13.5 us  [the longest x6 10 us: over_ao(): lax.ppermute(x, 'ao', [(i, i ^ k) for i in range(blocks)])]
    pallas_call x0 -> x4, Pallas kernels: none -> 10.8 us  [the longest x1 4.6 us: permuted_form(): pl.pallas_call(functools.partial(slot_sums, blocks, pairs, block), grid=(...]
    dot_general x2 -> x0, matrix products: 4.71 us -> none  [the longest x1 3.71 us: per_device(): jnp.dot(three_center.reshape(fit_dev * block, pairs * block), chosen, pre...]
    unnamed x0 -> x18, local copies, waits for them, and re-layouts: none -> 2.55 us
    pallas_call x0 -> x1, local copies, waits for them, and re-layouts: none -> 1.54 us  [permuted_form(): pl.pallas_call(finish, out_shape=jax.ShapeDtypeStruct((block, columns), j...]
  transfers between devices with their start and end apart: 1 -> 10, of which waited for: 1 -> 7; matrix products, arithmetic and copies ran while one was open for 0% -> 0% of each run, Pallas kernels for 0% -> 10%
where the time goes in v1:
time: 45.9 us; the launch traced here: 45.6 us
  waiting for transfers between devices  15 us (33%)
  starting transfers between devices  13.5 us (29%)
  Pallas kernels  10.8 us (24%)
  local copies, waits for them, and re-layouts  4.71 us (10%)
  other arithmetic  0.93 us (2%)
  between operations  0.69 us (2%)
    ppermute x6, waiting for transfers between devices, over_ao(): lax.ppermute(x, 'ao', [(i, i ^ k) for i in range(blocks)])  10.1 us
    ppermute x6, starting transfers between devices, over_ao(): lax.ppermute(x, 'ao', [(i, i ^ k) for i in range(blocks)])  10 us
    ppermute x4, waiting for transfers between devices, over_fit(): return lax.ppermute(x, 'fit', [(i, i ^ k) for i in range(2 * blocks)])  4.92 us
    pallas_call x1, Pallas kernels, permuted_form(): pl.pallas_call(functools.partial(slot_sums, blocks, pairs, block), grid=(...  4.6 us
    ppermute x4, starting transfers between devices, over_fit(): return lax.ppermute(x, 'fit', [(i, i ^ k) for i in range(2 * blocks)])  3.49 us
    unnamed x18, local copies, waits for them, and re-layouts  2.55 us
    pallas_call x1, Pallas kernels, permuted_form(): pl.pallas_call(functools.partial(transform, blocks), out_shape=jax.ShapeD...  2.36 us
    pallas_call x1, Pallas kernels, permuted_form(): pl.pallas_call(functools.partial(products, blocks, fits), out_shape=(piec...  2.29 us
  transfers between devices with their start and end apart: 10, of which 7 were waited for; matrix products, arithmetic and copies ran while one was open for 0% of the time, Pallas kernels for 10%

profile of v1, /device:TPU:0, one launch (start us, length us, event | category | flops | bytes accessed | tf_op | source)
XLA Modules:
  0.0 45.6 jit_solution(6319515530099090753)
XLA Ops:
  0.0 4.0 %collective-permute-start.1 = (bf16[128,128]{1,0:T(8,128)(2,1)}, bf16[128,128]{1,0:T(8,128)(2,1)S(1)}, u32[]{:S(2)}, u32[]{:S(2)}) collective-permute-start(bf16[128,128]{1,0:T(8,128)(2,1)} %refs_0_.1), channel_id=1, source_target_pairs={{0,16},{8,24},{16,0},{24,8},{1,17},{9,25},{17,1},{25,9},{2,18},{10... | collective-permute-start | bytes 98312 | tf_op jit(solution)/shard_map/ppermute | solution.py:97
  4.0 1.6 %collective-permute-start = (bf16[128,128]{1,0:T(8,128)(2,1)}, bf16[128,128]{1,0:T(8,128)(2,1)S(1)}, u32[]{:S(2)}, u32[]{:S(2)}) collective-permute-start(bf16[128,128]{1,0:T(8,128)(2,1)} %refs_0_.1), channel_id=1, source_target_pairs={{0,8},{8,0},{16,24},{24,16},{1,9},{9,1},{17,25},{25,17},{2,10},{10... | collective-permute-start | bytes 98312 | tf_op jit(solution)/shard_map/ppermute | solution.py:97
  5.6 0.0 collective-permute-start.2
  6.3 4.6 %slot_sums.1.sums_ref = bf16[512,1024]{1,0:T(8,128)(2,1)} custom-call(s32[1,32]{1,0:T(1,128)} %pair_ref.1, s32[1]{0:T(128)S(6)} %copy.6.count_ref, bf16[4,128,4096]{2,1,0:T(8,128)(2,1)} %x_ref.1), custom_call_target="tpu_custom_call" | custom-call | tf_op jit(solution)/shard_map/slot_sums/pallas_call | solution.py:103
  10.9 0.0 collective-permute-done.1.refs_2_
  10.9 0.0 copy-start.3
  10.9 0.0 collective-permute-done.refs_1_
  10.9 0.0 copy-start.4
  10.9 0.6 %collective-permute-done.2.refs_3_ = bf16[128,128]{1,0:T(8,128)(2,1)S(1)} collective-permute-done((bf16[128,128]{1,0:T(8,128)(2,1)}, bf16[128,128]{1,0:T(8,128)(2,1)S(1)}, u32[]{:S(2)}, u32[]{:S(2)}) %collective-permute-start.2) | collective-permute-done | bytes 32800 | tf_op jit(solution)/shard_map/ppermute | solution.py:97
  11.5 0.0 copy-done.3
  11.5 0.0 copy-done.4
  11.5 0.0 copy-start.5
  11.5 0.6 %copy-done.5 = bf16[128,128]{1,0:T(8,128)(2,1)} copy-done((bf16[128,128]{1,0:T(8,128)(2,1)}, bf16[128,128]{1,0:T(8,128)(2,1)S(1)}, u32[]{:S(2)}) %copy-start.5) | copy-done | bytes 32792
  12.1 2.4 %transform.1.refs_0_ = bf16[4,128,128]{2,1,0:T(8,128)(2,1)} custom-call(bf16[512,1024]{1,0:T(8,128)(2,1)} %slot_sums.1.sums_ref, bf16[128,128]{1,0:T(8,128)(2,1)} %refs_0_.1, bf16[128,128]{1,0:T(8,128)(2,1)} %copy-done.4, bf16[128,128]{1,0:T(8,128)(2,1)} %copy-done.3, bf16[128,128]{1,0:T(8,128)(2,1)} %copy-done.5), custom_call_target="tpu_custom_call" | custom-call | tf_op jit(solution)/shard_map/transform/pallas_call | solution.py:112
  14.5 3.4 %collective-permute-start.5 = (bf16[4,128,128]{2,1,0:T(8,128)(2,1)}, bf16[4,128,128]{2,1,0:T(8,128)(2,1)S(1)}, u32[]{:S(2)}, u32[]{:S(2)}) collective-permute-start(bf16[4,128,128]{2,1,0:T(8,128)(2,1)} %transform.1.refs_0_), channel_id=1, source_target_pairs={{0,24},{8,16},{16,8},{24,0},{1,25},{9,17},{17,9},{25,1},{2,26},{10... | collective-permute-start | bytes 393224 | tf_op jit(solution)/shard_map/ppermute | solution.py:97
  17.9 0.0 collective-permute-start.4
  17.9 0.9 %collective-permute-start.3 = (bf16[4,128,128]{2,1,0:T(8,128)(2,1)}, bf16[4,128,128]{2,1,0:T(8,128)(2,1)S(1)}, u32[]{:S(2)}, u32[]{:S(2)}) collective-permute-start(bf16[4,128,128]{2,1,0:T(8,128)(2,1)} %transform.1.refs_0_), channel_id=1, source_target_pairs={{0,8},{8,0},{16,24},{24,16},{1,9},{9,1},{17,25},{25,17},{2,10},{10... | collective-permute-start | bytes 393224 | tf_op jit(solution)/shard_map/ppermute | solution.py:97
  18.9 4.1 %collective-permute-done.5.refs_3_ = bf16[4,128,128]{2,1,0:T(8,128)(2,1)S(1)} collective-permute-done((bf16[4,128,128]{2,1,0:T(8,128)(2,1)}, bf16[4,128,128]{2,1,0:T(8,128)(2,1)S(1)}, u32[]{:S(2)}, u32[]{:S(2)}) %collective-permute-start.5) | collective-permute-done | bytes 131104 | tf_op jit(solution)/shard_map/ppermute | solution.py:97
  23.0 0.0 copy-start
  23.0 5.4 %collective-permute-done.4.refs_2_ = bf16[4,128,128]{2,1,0:T(8,128)(2,1)S(1)} collective-permute-done((bf16[4,128,128]{2,1,0:T(8,128)(2,1)}, bf16[4,128,128]{2,1,0:T(8,128)(2,1)S(1)}, u32[]{:S(2)}, u32[]{:S(2)}) %collective-permute-start.4) | collective-permute-done | bytes 131104 | tf_op jit(solution)/shard_map/ppermute | solution.py:97
  28.3 0.0 copy-start.1
  28.3 0.0 collective-permute-done.3.refs_1_
  28.3 0.0 copy-done
  28.3 0.7 %copy-done.1 = bf16[4,128,128]{2,1,0:T(8,128)(2,1)} copy-done((bf16[4,128,128]{2,1,0:T(8,128)(2,1)}, bf16[4,128,128]{2,1,0:T(8,128)(2,1)S(1)}, u32[]{:S(2)}) %copy-start.1) | copy-done | bytes 131096
  29.0 0.0 copy-start.2
  29.0 0.6 %copy-done.2 = bf16[4,128,128]{2,1,0:T(8,128)(2,1)} copy-done((bf16[4,128,128]{2,1,0:T(8,128)(2,1)}, bf16[4,128,128]{2,1,0:T(8,128)(2,1)S(1)}, u32[]{:S(2)}) %copy-start.2) | copy-done | bytes 131096
  29.6 2.3 %products.1 = (f32[4,64,128]{2,1,0:T(8,128)}, f32[4,64,128]{2,1,0:T(8,128)}) custom-call(bf16[4,128,128]{2,1,0:T(8,128)(2,1)} %transform.1.refs_0_, bf16[4,128,128]{2,1,0:T(8,128)(2,1)} %copy-done.2, bf16[4,128,128]{2,1,0:T(8,128)(2,1)} %copy-done.1, bf16[4,128,128]{2,1,0:T(8,128)(2,1)} %copy-done), custom_call_target="tpu_custom_call" | custom-call | tf_op jit(solution)/shard_map/products/pallas_call | solution.py:121
  31.9 0.0 collective-permute-start.6
  31.9 1.6 %collective-permute-done.6 = f32[4,64,128]{2,1,0:T(8,128)S(1)} collective-permute-done((f32[4,64,128]{2,1,0:T(8,128)}, f32[4,64,128]{2,1,0:T(8,128)S(1)}, u32[]{:S(2)}, u32[]{:S(2)}) %collective-permute-start.6) | collective-permute-done | bytes 131104 | tf_op jit(solution)/shard_map/ppermute | solution.py:100
  33.5 0.9 %add.3 = f32[4,64,128]{2,1,0:T(8,128)S(1)} add(f32[4,64,128]{2,1,0:T(8,128)} %get-tuple-element.7, f32[4,64,128]{2,1,0:T(8,128)S(1)} %collective-permute-done.6) | non-fusion elementwise | flops 32768 | bytes 393216 | tf_op jit(solution)/shard_map/add | solution.py:129
  34.4 0.6 %slice_bitcast_fusion = (f32[64,128]{1,0:T(8,128)S(1)}, f32[64,128]{1,0:T(8,128)S(1)}, f32[64,128]{1,0:T(8,128)S(1)}, f32[64,128]{1,0:T(8,128)}) fusion(f32[4,64,128]{2,1,0:T(8,128)S(1)} %add.3), kind=kLoop, calls=%fused_computation | loop fusion | bytes 262144 | tf_op jit(solution)/shard_map/squeeze | solution.py:130
  35.0 2.4 %collective-permute-start.9 = (f32[64,128]{1,0:T(8,128)S(1)}, f32[64,128]{1,0:T(8,128)S(1)}, u32[]{:S(2)}, u32[]{:S(2)}) collective-permute-start(f32[64,128]{1,0:T(8,128)S(1)} %get-tuple-element.9), channel_id=1, source_target_pairs={{0,6},{1,7},{2,4},{3,5},{4,2},{5,3},{6,0},{7,1},{8,14},{9,15},{10,... | collective-permute-start | bytes 98312 | tf_op jit(solution)/shard_map/ppermute | solution.py:100
  37.5 0.5 %collective-permute-start.8 = (f32[64,128]{1,0:T(8,128)S(1)}, f32[64,128]{1,0:T(8,128)S(1)}, u32[]{:S(2)}, u32[]{:S(2)}) collective-permute-start(f32[64,128]{1,0:T(8,128)S(1)} %get-tuple-element.10), channel_id=1, source_target_pairs={{0,4},{1,5},{2,6},{3,7},{4,0},{5,1},{6,2},{7,3},{8,12},{9,13},{10,... | collective-permute-start | bytes 98312 | tf_op jit(solution)/shard_map/ppermute | solution.py:100
  38.0 0.5 %collective-permute-start.7 = (f32[64,128]{1,0:T(8,128)S(1)}, f32[64,128]{1,0:T(8,128)S(1)}, u32[]{:S(2)}, u32[]{:S(2)}) collective-permute-start(f32[64,128]{1,0:T(8,128)S(1)} %get-tuple-element.11), channel_id=1, source_target_pairs={{0,2},{1,3},{2,0},{3,1},{4,6},{5,7},{6,4},{7,5},{8,10},{9,11},{10,... | collective-permute-start | bytes 98312 | tf_op jit(solution)/shard_map/ppermute | solution.py:100
  38.5 1.3 %collective-permute-done.9.refs_2_ = f32[64,128]{1,0:T(8,128)S(1)} collective-permute-done((f32[64,128]{1,0:T(8,128)S(1)}, f32[64,128]{1,0:T(8,128)S(1)}, u32[]{:S(2)}, u32[]{:S(2)}) %collective-permute-start.9) | collective-permute-done | bytes 32800 | tf_op jit(solution)/shard_map/ppermute | solution.py:100
  39.8 0.0 copy-start.6
  39.9 1.5 %collective-permute-done.8.refs_1_ = f32[64,128]{1,0:T(8,128)S(1)} collective-permute-done((f32[64,128]{1,0:T(8,128)S(1)}, f32[64,128]{1,0:T(8,128)S(1)}, u32[]{:S(2)}, u32[]{:S(2)}) %collective-permute-start.8) | collective-permute-done | bytes 32800 | tf_op jit(solution)/shard_map/ppermute | solution.py:100
  41.4 0.0 copy-start.7
  41.4 0.5 %collective-permute-done.7.refs_0_ = f32[64,128]{1,0:T(8,128)S(1)} collective-permute-done((f32[64,128]{1,0:T(8,128)S(1)}, f32[64,128]{1,0:T(8,128)S(1)}, u32[]{:S(2)}, u32[]{:S(2)}) %collective-permute-start.7) | collective-permute-done | bytes 32800 | tf_op jit(solution)/shard_map/ppermute | solution.py:100
  41.9 0.0 copy-start.8
  41.9 0.0 copy-done.6
  41.9 0.1 copy-done.7
  42.0 0.5 %copy-done.8 = f32[64,128]{1,0:T(8,128)} copy-done((f32[64,128]{1,0:T(8,128)}, f32[64,128]{1,0:T(8,128)S(1)}, u32[]{:S(2)}) %copy-start.8) | copy-done | bytes 32792
  42.5 1.5 %finish.1 = f32[128,64]{1,0:T(8,128)} custom-call(f32[64,128]{1,0:T(8,128)} %get-tuple-element.12.own_ref, f32[64,128]{1,0:T(8,128)} %copy-done.8, f32[64,128]{1,0:T(8,128)} %copy-done.7, f32[64,128]{1,0:T(8,128)} %copy-done.6), custom_call_target="tpu_custom_call" | custom-call | tf_op jit(solution)/shard_map/finish/pallas_call | solution.py:131
  44.0 1.5 %copy.5 = f32[128,64]{0,1:T(8,128)} copy(f32[128,64]{1,0:T(8,128)} %finish.1) | data formatting | bytes 65536 | tf_op jit(solution)/shard_map/finish/pallas_call | solution.py:131
Async XLA Ops:
  0.0 10.9 %collective-permute-start.1 = (bf16[128,128]{1,0:T(8,128)(2,1)}, bf16[128,128]{1,0:T(8,128)(2,1)S(1)}, u32[]{:S(2)}, u32[]{:S(2)}) collective-permute-start(bf16[128,128]{1,0:T(8,128)(2,1)} %refs_0_.1), channel_id=1, source_target_pairs={{0,16},{8,24},{16,0},{24,8},{1,17},{9,25},{17,1},{25,9},{2,18},{10... | collective-permute-start | bytes 98312 | tf_op jit(solution)/shard_map/ppermute | solution.py:97
  4.0 6.8 %collective-permute-start = (bf16[128,128]{1,0:T(8,128)(2,1)}, bf16[128,128]{1,0:T(8,128)(2,1)S(1)}, u32[]{:S(2)}, u32[]{:S(2)}) collective-permute-start(bf16[128,128]{1,0:T(8,128)(2,1)} %refs_0_.1), channel_id=1, source_target_pairs={{0,8},{8,0},{16,24},{24,16},{1,9},{9,1},{17,25},{25,17},{2,10},{10... | collective-permute-start | bytes 98312 | tf_op jit(solution)/shard_map/ppermute | solution.py:97
  5.6 5.9 %collective-permute-start.2 = (bf16[128,128]{1,0:T(8,128)(2,1)}, bf16[128,128]{1,0:T(8,128)(2,1)S(1)}, u32[]{:S(2)}, u32[]{:S(2)}) collective-permute-start(bf16[128,128]{1,0:T(8,128)(2,1)} %refs_0_.1), channel_id=1, source_target_pairs={{0,24},{8,16},{16,8},{24,0},{1,25},{9,17},{17,9},{25,1},{2,26},{10... | collective-permute-start | bytes 98312 | tf_op jit(solution)/shard_map/ppermute | solution.py:97
  10.9 0.7 %copy-start.3 = (bf16[128,128]{1,0:T(8,128)(2,1)}, bf16[128,128]{1,0:T(8,128)(2,1)S(1)}, u32[]{:S(2)}) copy-start(bf16[128,128]{1,0:T(8,128)(2,1)S(1)} %collective-permute-done.1.refs_2_) | copy-start | bytes 98308
  10.9 0.7 %copy-start.4 = (bf16[128,128]{1,0:T(8,128)(2,1)}, bf16[128,128]{1,0:T(8,128)(2,1)S(1)}, u32[]{:S(2)}) copy-start(bf16[128,128]{1,0:T(8,128)(2,1)S(1)} %collective-permute-done.refs_1_) | copy-start | bytes 98308
  11.5 0.6 %copy-start.5 = (bf16[128,128]{1,0:T(8,128)(2,1)}, bf16[128,128]{1,0:T(8,128)(2,1)S(1)}, u32[]{:S(2)}) copy-start(bf16[128,128]{1,0:T(8,128)(2,1)S(1)} %collective-permute-done.2.refs_3_) | copy-start | bytes 98308
  14.5 8.4 %collective-permute-start.5 = (bf16[4,128,128]{2,1,0:T(8,128)(2,1)}, bf16[4,128,128]{2,1,0:T(8,128)(2,1)S(1)}, u32[]{:S(2)}, u32[]{:S(2)}) collective-permute-start(bf16[4,128,128]{2,1,0:T(8,128)(2,1)} %transform.1.refs_0_), channel_id=1, source_target_pairs={{0,24},{8,16},{16,8},{24,0},{1,25},{9,17},{17,9},{25,1},{2,26},{10... | collective-permute-start | bytes 393224 | tf_op jit(solution)/shard_map/ppermute | solution.py:97
  17.9 10.4 %collective-permute-start.4 = (bf16[4,128,128]{2,1,0:T(8,128)(2,1)}, bf16[4,128,128]{2,1,0:T(8,128)(2,1)S(1)}, u32[]{:S(2)}, u32[]{:S(2)}) collective-permute-start(bf16[4,128,128]{2,1,0:T(8,128)(2,1)} %transform.1.refs_0_), channel_id=1, source_target_pairs={{0,16},{8,24},{16,0},{24,8},{1,17},{9,25},{17,1},{25,9},{2,18},{10... | collective-permute-start | bytes 393224 | tf_op jit(solution)/shard_map/ppermute | solution.py:97
  17.9 10.4 %collective-permute-start.3 = (bf16[4,128,128]{2,1,0:T(8,128)(2,1)}, bf16[4,128,128]{2,1,0:T(8,128)(2,1)S(1)}, u32[]{:S(2)}, u32[]{:S(2)}) collective-permute-start(bf16[4,128,128]{2,1,0:T(8,128)(2,1)} %transform.1.refs_0_), channel_id=1, source_target_pairs={{0,8},{8,0},{16,24},{24,16},{1,9},{9,1},{17,25},{25,17},{2,10},{10... | collective-permute-start | bytes 393224 | tf_op jit(solution)/shard_map/ppermute | solution.py:97
  23.0 5.4 %copy-start = (bf16[4,128,128]{2,1,0:T(8,128)(2,1)}, bf16[4,128,128]{2,1,0:T(8,128)(2,1)S(1)}, u32[]{:S(2)}) copy-start(bf16[4,128,128]{2,1,0:T(8,128)(2,1)S(1)} %collective-permute-done.5.refs_3_) | copy-start | bytes 393220
  28.3 0.7 %copy-start.1 = (bf16[4,128,128]{2,1,0:T(8,128)(2,1)}, bf16[4,128,128]{2,1,0:T(8,128)(2,1)S(1)}, u32[]{:S(2)}) copy-start(bf16[4,128,128]{2,1,0:T(8,128)(2,1)S(1)} %collective-permute-done.4.refs_2_) | copy-start | bytes 393220
  29.0 0.6 %copy-start.2 = (bf16[4,128,128]{2,1,0:T(8,128)(2,1)}, bf16[4,128,128]{2,1,0:T(8,128)(2,1)S(1)}, u32[]{:S(2)}) copy-start(bf16[4,128,128]{2,1,0:T(8,128)(2,1)S(1)} %collective-permute-done.3.refs_1_) | copy-start | bytes 393220
  31.9 1.6 %collective-permute-start.6 = (f32[4,64,128]{2,1,0:T(8,128)}, f32[4,64,128]{2,1,0:T(8,128)S(1)}, u32[]{:S(2)}, u32[]{:S(2)}) collective-permute-start(f32[4,64,128]{2,1,0:T(8,128)} %get-tuple-element.8), channel_id=1, source_target_pairs={{0,1},{1,0},{2,3},{3,2},{4,5},{5,4},{6,7},{7,6},{8,9},{9,8},{10,11... | collective-permute-start | bytes 393224 | tf_op jit(solution)/shard_map/ppermute | solution.py:100
  35.0 4.8 %collective-permute-start.9 = (f32[64,128]{1,0:T(8,128)S(1)}, f32[64,128]{1,0:T(8,128)S(1)}, u32[]{:S(2)}, u32[]{:S(2)}) collective-permute-start(f32[64,128]{1,0:T(8,128)S(1)} %get-tuple-element.9), channel_id=1, source_target_pairs={{0,6},{1,7},{2,4},{3,5},{4,2},{5,3},{6,0},{7,1},{8,14},{9,15},{10,... | collective-permute-start | bytes 98312 | tf_op jit(solution)/shard_map/ppermute | solution.py:100
  37.5 3.9 %collective-permute-start.8 = (f32[64,128]{1,0:T(8,128)S(1)}, f32[64,128]{1,0:T(8,128)S(1)}, u32[]{:S(2)}, u32[]{:S(2)}) collective-permute-start(f32[64,128]{1,0:T(8,128)S(1)} %get-tuple-element.10), channel_id=1, source_target_pairs={{0,4},{1,5},{2,6},{3,7},{4,0},{5,1},{6,2},{7,3},{8,12},{9,13},{10,... | collective-permute-start | bytes 98312 | tf_op jit(solution)/shard_map/ppermute | solution.py:100
  38.0 3.9 %collective-permute-start.7 = (f32[64,128]{1,0:T(8,128)S(1)}, f32[64,128]{1,0:T(8,128)S(1)}, u32[]{:S(2)}, u32[]{:S(2)}) collective-permute-start(f32[64,128]{1,0:T(8,128)S(1)} %get-tuple-element.11), channel_id=1, source_target_pairs={{0,2},{1,3},{2,0},{3,1},{4,6},{5,7},{6,4},{7,5},{8,10},{9,11},{10,... | collective-permute-start | bytes 98312 | tf_op jit(solution)/shard_map/ppermute | solution.py:100
  39.8 2.1 %copy-start.6 = (f32[64,128]{1,0:T(8,128)}, f32[64,128]{1,0:T(8,128)S(1)}, u32[]{:S(2)}) copy-start(f32[64,128]{1,0:T(8,128)S(1)} %collective-permute-done.9.refs_2_) | copy-start | bytes 98308
  41.4 0.6 %copy-start.7 = (f32[64,128]{1,0:T(8,128)}, f32[64,128]{1,0:T(8,128)S(1)}, u32[]{:S(2)}) copy-start(f32[64,128]{1,0:T(8,128)S(1)} %collective-permute-done.8.refs_1_) | copy-start | bytes 98308
  41.9 0.6 %copy-start.8 = (f32[64,128]{1,0:T(8,128)}, f32[64,128]{1,0:T(8,128)S(1)}, u32[]{:S(2)}) copy-start(f32[64,128]{1,0:T(8,128)S(1)} %collective-permute-done.7.refs_0_) | copy-start | bytes 98308

commit v2 on v1

--- a/solution.py
+++ b/solution.py
@@ -8,7 +8,9 @@
 from jax.sharding import PartitionSpec as P
 
 VMEM = pl.BlockSpec(memory_space=pltpu.VMEM)
+HBM = pl.BlockSpec(memory_space=pltpu.HBM)
 SMEM = pl.BlockSpec(memory_space=pltpu.SMEM)
+TOGETHER = 4
 
 
 def gathered_form(coefficients, three_center, pair_blocks, pair_count):
@@ -35,21 +37,53 @@
     return lax.psum_scatter(terms, "fit", scatter_dimension=1, tiled=True)
 
 
-def slot_sums(blocks, pairs, width, pair_ref, count_ref, x_ref, sums_ref, acc):
+def slot_sums(blocks, pair_ref, count_ref, x_ref, sums_ref, buffer, arrived, pairs_here, listed, order, counts):
+    fits, block, wide = x_ref.shape
+    pairs = pair_ref.shape[1]
+    slots = pltpu.make_async_copy(pair_ref, pairs_here, listed)
+    slots.start()
+    copies = [
+        pltpu.make_async_copy(x_ref.at[i], buffer.at[i, :, pl.ds(0, wide)], arrived.at[i]) for i in range(fits)
+    ]
+    for copy in copies:
+        copy.start()
+    buffer[:, :, wide:] = jnp.zeros((fits, block, block), buffer.dtype)
     z = lax.axis_index("ao")
-    acc[...] = jnp.zeros_like(acc)
+    for place in range(blocks):
+        counts[place] = 0
+    slots.wait()
 
-    def add(p, carry):
-        place = pair_ref[0, p] ^ z
-        acc[place] += x_ref[0, :, pl.ds(pl.multiple_of(p * width, width), width)].astype(jnp.float32)
+    def enlist(p, carry):
+        place = pairs_here[0, p] ^ z
+        n = counts[place]
+        order[place, n] = p
+        counts[place] = n + 1
         return carry
 
-    lax.fori_loop(0, jnp.minimum(count_ref[0], pairs), add, 0)
-    for b in range(blocks):
-        whole = acc[b]
-        high = whole.astype(jnp.bfloat16)
-        sums_ref[:, b * width : (b + 1) * width] = high
-        sums_ref[:, (blocks + b) * width : (blocks + b + 1) * width] = (whole - high.astype(jnp.float32)).astype(jnp.bfloat16)
+    lax.fori_loop(0, jnp.minimum(count_ref[0], pairs), enlist, 0)
+    for place in range(blocks):
+        n = counts[place]
+        for j in range(TOGETHER - 1):
+            order[place, n + j] = pairs
+    for i in range(fits):
+        copies[i].wait()
+        for place in range(blocks):
+
+            def slot(s):
+                start = pl.multiple_of(order[place, s] * block, block)
+                return buffer[i, :, pl.ds(start, block)].astype(jnp.float32)
+
+            def add(s, total):
+                s = s * TOGETHER
+                return total + ((slot(s) + slot(s + 1)) + (slot(s + 2) + slot(s + 3)))
+
+            rounds = (counts[place] + TOGETHER - 1) // TOGETHER
+            whole = lax.fori_loop(0, rounds, add, jnp.zeros((block, block), jnp.float32))
+            high = whole.astype(jnp.bfloat16)
+            low = (whole - high.astype(jnp.float32)).astype(jnp.bfloat16)
+            rows = slice(i * block, (i + 1) * block)
+            sums_ref[rows, place * block : (place + 1) * block] = high
+            sums_ref[rows, (blocks + place) * block : (blocks + place + 1) * block] = low
 
 
 def transform(blocks, sums_ref, *refs):
@@ -78,14 +112,6 @@
         send_ref[place] = whole[k, pl.ds(pl.multiple_of((1 - core) * columns, columns), columns), :]
 
 
-def finish(own_ref, *refs):
-    out_ref = refs[-1]
-    total = own_ref[...]
-    for ref in refs[:-1]:
-        total = total + ref[...]
-    out_ref[...] = total.T
-
-
 def permuted_form(blocks, coefficients, three_center, pair_blocks, pair_count):
     fits, block, wide = three_center.shape
     pairs = pair_blocks.shape[1]
@@ -99,25 +125,38 @@
     def over_fit(x, k):
         return lax.ppermute(x, "fit", [(i, i ^ k) for i in range(2 * blocks)])
 
+    def held(x):
+        return pltpu.with_memory_space_constraint(x, pltpu.VMEM)
+
+    def far(x):
+        return pltpu.with_memory_space_constraint(x, pltpu.HBM)
+
     coefs = [coefficients] + over_ao(coefficients)
     sums = pl.pallas_call(
-        functools.partial(slot_sums, blocks, pairs, block),
-        grid=(fits,),
-        out_shape=jax.ShapeDtypeStruct((fits * block, 2 * blocks * block), jnp.bfloat16),
-        in_specs=[SMEM, SMEM, pl.BlockSpec((1, block, wide), lambda i: (i, 0, 0))],
-        out_specs=pl.BlockSpec((block, 2 * blocks * block), lambda i: (i, 0)),
-        scratch_shapes=[pltpu.VMEM((blocks, block, block), jnp.float32)],
+        functools.partial(slot_sums, blocks),
+        out_shape=pltpu.VMEM((fits * block, 2 * blocks * block), jnp.bfloat16),
+        in_specs=[HBM, SMEM, HBM],
+        out_specs=VMEM,
+        scratch_shapes=[
+            pltpu.VMEM((fits, block, wide + block), jnp.bfloat16),
+            pltpu.SemaphoreType.DMA((fits,)),
+            pltpu.SMEM((1, pairs), jnp.int32),
+            pltpu.SemaphoreType.DMA,
+            pltpu.SMEM((blocks, pairs + TOGETHER), jnp.int32),
+            pltpu.SMEM((blocks,), jnp.int32),
+        ],
+        compiler_params=pltpu.CompilerParams(vmem_limit_bytes=32 << 20),
         name="slot_sums",
-    )(pair_blocks, pair_count, three_center)
+    )(far(pair_blocks), pair_count, far(three_center))
     half = pl.pallas_call(
         functools.partial(transform, blocks),
-        out_shape=jax.ShapeDtypeStruct((fits, block, orbitals), jnp.bfloat16),
+        out_shape=pltpu.VMEM((fits, block, orbitals), jnp.bfloat16),
         in_specs=[VMEM] * (blocks + 1),
         out_specs=VMEM,
         name="transform",
-    )(sums, *coefs)
+    )(held(sums), *[held(x) for x in coefs])
     halves = [half] + over_ao(half)
-    piece = jax.ShapeDtypeStruct((blocks, columns, block), jnp.float32)
+    piece = pltpu.VMEM((blocks, columns, block), jnp.float32)
     keep, send = pl.pallas_call(
         functools.partial(products, blocks, fits),
         out_shape=(piece, piece),
@@ -125,16 +164,12 @@
         out_specs=(VMEM, VMEM),
         scratch_shapes=[pltpu.VMEM((blocks, block, block), jnp.float32)],
         name="products",
-    )(*halves)
+    )(*[held(x) for x in halves])
     chip = keep + over_fit(send, 1)
-    parts = [chip[0]] + [over_fit(chip[k], 2 * k) for k in chips]
-    return pl.pallas_call(
-        finish,
-        out_shape=jax.ShapeDtypeStruct((block, columns), jnp.float32),
-        in_specs=[VMEM] * blocks,
-        out_specs=VMEM,
-        name="finish",
-    )(*parts)
+    total = chip[0]
+    for k in chips:
+        total = total + over_fit(chip[k], 2 * k)
+    return total.T
 
 
 def solution(mesh):

time: 45.9 us -> 33.6 us (0.73)
  Pallas kernels: 10.8 us -> 3.28 us
  local copies, waits for them, and re-layouts: 4.71 us -> 0.01 us
    pallas_call x3 -> x2, Pallas kernels: 8.48 us -> 2.78 us  [the longest x1 2.34 us: permuted_form(): pl.pallas_call(functools.partial(slot_sums, blocks), out_shape=pltpu.VMEM...]
    unnamed x18 -> x2, local copies, waits for them, and re-layouts: 2.55 us -> 0.01 us
    pallas_call x1, Pallas kernels: 2.29 us -> 0.5 us  [permuted_form(): pl.pallas_call(functools.partial(products, blocks, fits), out_shape=(piec...]
    pallas_call x1 -> x0, local copies, waits for them, and re-layouts: 1.54 us -> none  [permuted_form(): pl.pallas_call(finish, out_shape=jax.ShapeDtypeStruct((block, columns), j...]
    add x1, other arithmetic: 0.93 us -> 0.02 us  [permuted_form(): chip = keep + over_fit(send, 1)]
    transpose x0 -> x1, other arithmetic: none -> 0.62 us  [permuted_form(): return total.T]
    squeeze x1, local copies, waits for them, and re-layouts: 0.63 us -> 0.01 us  [permuted_form(): total = total + over_fit(chip[k], 2 * k)]
  transfers between devices with their start and end apart: 10 -> 10, of which waited for: 7 -> 7; matrix products, arithmetic and copies ran while one was open for 0% -> 0% of each run, Pallas kernels for 10% -> 7%
where the time goes in v2:
time: 33.6 us; the launch traced here: 33.4 us
  waiting for transfers between devices  15.1 us (45%)
  starting transfers between devices  13.7 us (41%)
  Pallas kernels  3.28 us (10%)
  between operations  0.72 us (2%)
  other arithmetic  0.65 us (2%)
    ppermute x6, waiting for transfers between devices, over_ao(): lax.ppermute(x, 'ao', [(i, i ^ k) for i in range(blocks)])  10.3 us
    ppermute x6, starting transfers between devices, over_ao(): lax.ppermute(x, 'ao', [(i, i ^ k) for i in range(blocks)])  10.1 us
    ppermute x4, waiting for transfers between devices, over_fit(): return lax.ppermute(x, 'fit', [(i, i ^ k) for i in range(2 * blocks)])  4.75 us
    ppermute x4, starting transfers between devices, over_fit(): return lax.ppermute(x, 'fit', [(i, i ^ k) for i in range(2 * blocks)])  3.62 us
    pallas_call x1, Pallas kernels, permuted_form(): pl.pallas_call(functools.partial(slot_sums, blocks), out_shape=pltpu.VMEM...  2.34 us
  transfers between devices with their start and end apart: 10, of which 7 were waited for; matrix products, arithmetic and copies ran while one was open for 0% of the time, Pallas kernels for 7%

profile of v2, /device:TPU:0, one launch (start us, length us, event | category | flops | bytes accessed | tf_op | source)
XLA Modules:
  0.0 33.4 jit_solution(9415708412463659910)
XLA Ops:
  0.0 0.0 copy-start
  0.0 4.0 %collective-permute-start.1 = (bf16[128,128]{1,0:T(8,128)(2,1)}, bf16[128,128]{1,0:T(8,128)(2,1)S(1)}, u32[]{:S(2)}, u32[]{:S(2)}) collective-permute-start(bf16[128,128]{1,0:T(8,128)(2,1)} %refs_0_.1), channel_id=1, source_target_pairs={{0,16},{8,24},{16,0},{24,8},{1,17},{9,25},{17,1},{25,9},{2,18},{10... | collective-permute-start | bytes 98312 | tf_op jit(solution)/shard_map/ppermute | solution.py:123
  4.0 1.6 %collective-permute-start = (bf16[128,128]{1,0:T(8,128)(2,1)}, bf16[128,128]{1,0:T(8,128)(2,1)S(1)}, u32[]{:S(2)}, u32[]{:S(2)}) collective-permute-start(bf16[128,128]{1,0:T(8,128)(2,1)} %refs_0_.1), channel_id=1, source_target_pairs={{0,8},{8,0},{16,24},{24,16},{1,9},{9,1},{17,25},{25,17},{2,10},{10... | collective-permute-start | bytes 98312 | tf_op jit(solution)/shard_map/ppermute | solution.py:123
  5.6 0.0 collective-permute-start.2
  6.3 2.3 %slot_sums.1.sums_ref = bf16[512,1024]{1,0:T(8,128)(2,1)S(1)} custom-call(s32[1,32]{1,0:T(1,128)} %pair_ref.1, s32[1]{0:T(128)S(6)} %copy.5.count_ref, bf16[4,128,4096]{2,1,0:T(8,128)(2,1)} %x_ref.1), custom_call_target="tpu_custom_call" | custom-call | tf_op jit(solution)/shard_map/slot_sums/pallas_call | solution.py:135
  8.6 0.0 collective-permute-done.1.refs_2_
  8.6 0.0 collective-permute-done.refs_1_
  8.6 2.9 %collective-permute-done.2.refs_3_ = bf16[128,128]{1,0:T(8,128)(2,1)S(1)} collective-permute-done((bf16[128,128]{1,0:T(8,128)(2,1)}, bf16[128,128]{1,0:T(8,128)(2,1)S(1)}, u32[]{:S(2)}, u32[]{:S(2)}) %collective-permute-start.2) | collective-permute-done | bytes 32800 | tf_op jit(solution)/shard_map/ppermute | solution.py:123
  11.6 0.0 copy-done
  11.6 0.4 %transform.1.refs_0_ = bf16[4,128,128]{2,1,0:T(8,128)(2,1)S(1)} custom-call(bf16[512,1024]{1,0:T(8,128)(2,1)S(1)} %slot_sums.1.sums_ref, bf16[128,128]{1,0:T(8,128)(2,1)S(1)} %copy-done, bf16[128,128]{1,0:T(8,128)(2,1)S(1)} %collective-permute-done.refs_1_, bf16[128,128]{1,0:T(8,128)(2,1)S(1)} %collective-permute-done.1.refs_2_, ...), custom_call_target="tpu_custom_call" | custom-call | tf_op jit(solution)/shard_map/transform/pallas_call | solution.py:151
  12.0 1.0 %collective-permute-start.5 = (bf16[4,128,128]{2,1,0:T(8,128)(2,1)S(1)}, bf16[4,128,128]{2,1,0:T(8,128)(2,1)S(1)}, u32[]{:S(2)}, u32[]{:S(2)}) collective-permute-start(bf16[4,128,128]{2,1,0:T(8,128)(2,1)S(1)} %transform.1.refs_0_), channel_id=1, source_target_pairs={{0,24},{8,16},{16,8},{24,0},{1,25},{9,17},{17,9},{25,1},{2,26},{10... | collective-permute-start | bytes 393224 | tf_op jit(solution)/shard_map/ppermute | solution.py:123
  13.0 0.0 collective-permute-start.4
  13.0 3.4 %collective-permute-start.3 = (bf16[4,128,128]{2,1,0:T(8,128)(2,1)S(1)}, bf16[4,128,128]{2,1,0:T(8,128)(2,1)S(1)}, u32[]{:S(2)}, u32[]{:S(2)}) collective-permute-start(bf16[4,128,128]{2,1,0:T(8,128)(2,1)S(1)} %transform.1.refs_0_), channel_id=1, source_target_pairs={{0,8},{8,0},{16,24},{24,16},{1,9},{9,1},{17,25},{25,17},{2,10},{10... | collective-permute-start | bytes 393224 | tf_op jit(solution)/shard_map/ppermute | solution.py:123
  16.4 3.8 %collective-permute-done.5.refs_3_ = bf16[4,128,128]{2,1,0:T(8,128)(2,1)S(1)} collective-permute-done((bf16[4,128,128]{2,1,0:T(8,128)(2,1)S(1)}, bf16[4,128,128]{2,1,0:T(8,128)(2,1)S(1)}, u32[]{:S(2)}, u32[]{:S(2)}) %collective-permute-start.5) | collective-permute-done | bytes 131104 | tf_op jit(solution)/shard_map/ppermute | solution.py:123
  20.3 3.6 %collective-permute-done.4.refs_2_ = bf16[4,128,128]{2,1,0:T(8,128)(2,1)S(1)} collective-permute-done((bf16[4,128,128]{2,1,0:T(8,128)(2,1)S(1)}, bf16[4,128,128]{2,1,0:T(8,128)(2,1)S(1)}, u32[]{:S(2)}, u32[]{:S(2)}) %collective-permute-start.4) | collective-permute-done | bytes 131104 | tf_op jit(solution)/shard_map/ppermute | solution.py:123
  23.9 0.0 collective-permute-done.3.refs_1_
  23.9 0.5 %products.1 = (f32[4,64,128]{2,1,0:T(8,128)S(1)}, f32[4,64,128]{2,1,0:T(8,128)S(1)}) custom-call(bf16[4,128,128]{2,1,0:T(8,128)(2,1)S(1)} %transform.1.refs_0_, bf16[4,128,128]{2,1,0:T(8,128)(2,1)S(1)} %collective-permute-done.3.refs_1_, bf16[4,128,128]{2,1,0:T(8,128)(2,1)S(1)} %collective-permute-done.4.refs_2_, ...), custom_call_target="tpu_custom_call" | custom-call | tf_op jit(solution)/shard_map/products/pallas_call | solution.py:160
  24.4 0.1 collective-permute-start.6
  24.5 1.3 %collective-permute-done.6 = f32[4,64,128]{2,1,0:T(8,128)S(1)} collective-permute-done((f32[4,64,128]{2,1,0:T(8,128)S(1)}, f32[4,64,128]{2,1,0:T(8,128)S(1)}, u32[]{:S(2)}, u32[]{:S(2)}) %collective-permute-start.6) | collective-permute-done | bytes 131104 | tf_op jit(solution)/shard_map/ppermute | solution.py:126
  25.8 1.6 %collective-permute-start.7 = (f32[64,128]{1,0:T(8,128)S(1)}, f32[64,128]{1,0:T(8,128)S(1)}, u32[]{:S(2)}, u32[]{:S(2)}) collective-permute-start(f32[64,128]{1,0:T(8,128)S(1)} %get-tuple-element.9), channel_id=1, source_target_pairs={{0,2},{1,3},{2,0},{3,1},{4,6},{5,7},{6,4},{7,5},{8,10},{9,11},{10,... | collective-permute-start | bytes 98312 | tf_op jit(solution)/shard_map/ppermute | solution.py:126
  27.4 1.5 %collective-permute-start.9 = (f32[64,128]{1,0:T(8,128)S(1)}, f32[64,128]{1,0:T(8,128)S(1)}, u32[]{:S(2)}, u32[]{:S(2)}) collective-permute-start(f32[64,128]{1,0:T(8,128)S(1)} %get-tuple-element.10), channel_id=1, source_target_pairs={{0,6},{1,7},{2,4},{3,5},{4,2},{5,3},{6,0},{7,1},{8,14},{9,15},{10,... | collective-permute-start | bytes 98312 | tf_op jit(solution)/shard_map/ppermute | solution.py:126
  28.9 0.5 %collective-permute-start.8 = (f32[64,128]{1,0:T(8,128)S(1)}, f32[64,128]{1,0:T(8,128)S(1)}, u32[]{:S(2)}, u32[]{:S(2)}) collective-permute-start(f32[64,128]{1,0:T(8,128)S(1)} %get-tuple-element.11), channel_id=1, source_target_pairs={{0,4},{1,5},{2,6},{3,7},{4,0},{5,1},{6,2},{7,3},{8,12},{9,13},{10,... | collective-permute-start | bytes 98312 | tf_op jit(solution)/shard_map/ppermute | solution.py:126
  29.4 0.4 %collective-permute-done.7 = f32[64,128]{1,0:T(8,128)S(1)} collective-permute-done((f32[64,128]{1,0:T(8,128)S(1)}, f32[64,128]{1,0:T(8,128)S(1)}, u32[]{:S(2)}, u32[]{:S(2)}) %collective-permute-start.7) | collective-permute-done | bytes 32800 | tf_op jit(solution)/shard_map/ppermute | solution.py:126
  29.8 2.4 %collective-permute-done.9 = f32[64,128]{1,0:T(8,128)S(1)} collective-permute-done((f32[64,128]{1,0:T(8,128)S(1)}, f32[64,128]{1,0:T(8,128)S(1)}, u32[]{:S(2)}, u32[]{:S(2)}) %collective-permute-start.9) | collective-permute-done | bytes 32800 | tf_op jit(solution)/shard_map/ppermute | solution.py:126
  32.2 0.6 %collective-permute-done.8 = f32[64,128]{1,0:T(8,128)S(1)} collective-permute-done((f32[64,128]{1,0:T(8,128)S(1)}, f32[64,128]{1,0:T(8,128)S(1)}, u32[]{:S(2)}, u32[]{:S(2)}) %collective-permute-start.8) | collective-permute-done | bytes 32800 | tf_op jit(solution)/shard_map/ppermute | solution.py:126
  32.8 0.6 %fusion.3 = f32[128,64]{0,1:T(8,128)} fusion(f32[64,128]{1,0:T(8,128)S(1)} %collective-permute-done.9, f32[64,128]{1,0:T(8,128)S(1)} %collective-permute-done.8, f32[64,128]{1,0:T(8,128)S(1)} %collective-permute-done.7, f32[4,64,128]{2,1,0:T(8,128)S(1)} %add.12), kind=kLoop, calls=%fused_computation.7 | loop fusion | flops 24576 | bytes 163840 | tf_op jit(solution)/shard_map/transpose | solution.py:172
  (2 shorter events, 0.0 us)
Async XLA Ops:
  0.0 11.6 %copy-start = (bf16[128,128]{1,0:T(8,128)(2,1)S(1)}, bf16[128,128]{1,0:T(8,128)(2,1)}, u32[]{:S(2)}) copy-start(bf16[128,128]{1,0:T(8,128)(2,1)} %refs_0_.1) | copy-start | bytes 98308
  0.0 8.6 %collective-permute-start.1 = (bf16[128,128]{1,0:T(8,128)(2,1)}, bf16[128,128]{1,0:T(8,128)(2,1)S(1)}, u32[]{:S(2)}, u32[]{:S(2)}) collective-permute-start(bf16[128,128]{1,0:T(8,128)(2,1)} %refs_0_.1), channel_id=1, source_target_pairs={{0,16},{8,24},{16,0},{24,8},{1,17},{9,25},{17,1},{25,9},{2,18},{10... | collective-permute-start | bytes 98312 | tf_op jit(solution)/shard_map/ppermute | solution.py:123
  4.0 4.6 %collective-permute-start = (bf16[128,128]{1,0:T(8,128)(2,1)}, bf16[128,128]{1,0:T(8,128)(2,1)S(1)}, u32[]{:S(2)}, u32[]{:S(2)}) collective-permute-start(bf16[128,128]{1,0:T(8,128)(2,1)} %refs_0_.1), channel_id=1, source_target_pairs={{0,8},{8,0},{16,24},{24,16},{1,9},{9,1},{17,25},{25,17},{2,10},{10... | collective-permute-start | bytes 98312 | tf_op jit(solution)/shard_map/ppermute | solution.py:123
  5.6 5.9 %collective-permute-start.2 = (bf16[128,128]{1,0:T(8,128)(2,1)}, bf16[128,128]{1,0:T(8,128)(2,1)S(1)}, u32[]{:S(2)}, u32[]{:S(2)}) collective-permute-start(bf16[128,128]{1,0:T(8,128)(2,1)} %refs_0_.1), channel_id=1, source_target_pairs={{0,24},{8,16},{16,8},{24,0},{1,25},{9,17},{17,9},{25,1},{2,26},{10... | collective-permute-start | bytes 98312 | tf_op jit(solution)/shard_map/ppermute | solution.py:123
  12.0 8.3 %collective-permute-start.5 = (bf16[4,128,128]{2,1,0:T(8,128)(2,1)S(1)}, bf16[4,128,128]{2,1,0:T(8,128)(2,1)S(1)}, u32[]{:S(2)}, u32[]{:S(2)}) collective-permute-start(bf16[4,128,128]{2,1,0:T(8,128)(2,1)S(1)} %transform.1.refs_0_), channel_id=1, source_target_pairs={{0,24},{8,16},{16,8},{24,0},{1,25},{9,17},{17,9},{25,1},{2,26},{10... | collective-permute-start | bytes 393224 | tf_op jit(solution)/shard_map/ppermute | solution.py:123
  13.0 10.9 %collective-permute-start.4 = (bf16[4,128,128]{2,1,0:T(8,128)(2,1)S(1)}, bf16[4,128,128]{2,1,0:T(8,128)(2,1)S(1)}, u32[]{:S(2)}, u32[]{:S(2)}) collective-permute-start(bf16[4,128,128]{2,1,0:T(8,128)(2,1)S(1)} %transform.1.refs_0_), channel_id=1, source_target_pairs={{0,16},{8,24},{16,0},{24,8},{1,17},{9,25},{17,1},{25,9},{2,18},{10... | collective-permute-start | bytes 393224 | tf_op jit(solution)/shard_map/ppermute | solution.py:123
  13.0 10.9 %collective-permute-start.3 = (bf16[4,128,128]{2,1,0:T(8,128)(2,1)S(1)}, bf16[4,128,128]{2,1,0:T(8,128)(2,1)S(1)}, u32[]{:S(2)}, u32[]{:S(2)}) collective-permute-start(bf16[4,128,128]{2,1,0:T(8,128)(2,1)S(1)} %transform.1.refs_0_), channel_id=1, source_target_pairs={{0,8},{8,0},{16,24},{24,16},{1,9},{9,1},{17,25},{25,17},{2,10},{10... | collective-permute-start | bytes 393224 | tf_op jit(solution)/shard_map/ppermute | solution.py:123
  24.4 1.4 %collective-permute-start.6 = (f32[4,64,128]{2,1,0:T(8,128)S(1)}, f32[4,64,128]{2,1,0:T(8,128)S(1)}, u32[]{:S(2)}, u32[]{:S(2)}) collective-permute-start(f32[4,64,128]{2,1,0:T(8,128)S(1)} %get-tuple-element.8), channel_id=1, source_target_pairs={{0,1},{1,0},{2,3},{3,2},{4,5},{5,4},{6,7},{7,6},{8,9},{9,8},{10,11... | collective-permute-start | bytes 393224 | tf_op jit(solution)/shard_map/ppermute | solution.py:126
  25.8 4.0 %collective-permute-start.7 = (f32[64,128]{1,0:T(8,128)S(1)}, f32[64,128]{1,0:T(8,128)S(1)}, u32[]{:S(2)}, u32[]{:S(2)}) collective-permute-start(f32[64,128]{1,0:T(8,128)S(1)} %get-tuple-element.9), channel_id=1, source_target_pairs={{0,2},{1,3},{2,0},{3,1},{4,6},{5,7},{6,4},{7,5},{8,10},{9,11},{10,... | collective-permute-start | bytes 98312 | tf_op jit(solution)/shard_map/ppermute | solution.py:126
  27.4 4.8 %collective-permute-start.9 = (f32[64,128]{1,0:T(8,128)S(1)}, f32[64,128]{1,0:T(8,128)S(1)}, u32[]{:S(2)}, u32[]{:S(2)}) collective-permute-start(f32[64,128]{1,0:T(8,128)S(1)} %get-tuple-element.10), channel_id=1, source_target_pairs={{0,6},{1,7},{2,4},{3,5},{4,2},{5,3},{6,0},{7,1},{8,14},{9,15},{10,... | collective-permute-start | bytes 98312 | tf_op jit(solution)/shard_map/ppermute | solution.py:126
  28.9 3.9 %collective-permute-start.8 = (f32[64,128]{1,0:T(8,128)S(1)}, f32[64,128]{1,0:T(8,128)S(1)}, u32[]{:S(2)}, u32[]{:S(2)}) collective-permute-start(f32[64,128]{1,0:T(8,128)S(1)} %get-tuple-element.11), channel_id=1, source_target_pairs={{0,4},{1,5},{2,6},{3,7},{4,0},{5,1},{6,2},{7,3},{8,12},{9,13},{10,... | collective-permute-start | bytes 98312 | tf_op jit(solution)/shard_map/ppermute | solution.py:126

commit v3 on v2

--- a/solution.py
+++ b/solution.py
@@ -11,6 +11,11 @@
 HBM = pl.BlockSpec(memory_space=pltpu.HBM)
 SMEM = pl.BlockSpec(memory_space=pltpu.SMEM)
 TOGETHER = 4
+ROUNDS = (
+    (4, 3, 0, 1, 5, 9, 13, 6, 11, 10, 2, 8, 15, 14, 12, 7),
+    (12, 0, 4, 8, 9, 13, 5, 1, 10, 2, 14, 6, 7, 3, 15, 11),
+    (8, 2, 12, 0, 7, 1, 4, 5, 9, 14, 6, 10, 11, 15, 13, 3),
+)
 
 
 def gathered_form(coefficients, three_center, pair_blocks, pair_count):
@@ -86,30 +91,61 @@
             sums_ref[rows, (blocks + place) * block : (blocks + place + 1) * block] = low
 
 
-def transform(blocks, sums_ref, *refs):
-    half_ref = refs[-1]
-    coefficients = jnp.concatenate([ref[...] for ref in refs[:-1]] * 2, axis=0)
+def transform(sums_ref, own_ref, near_ref, first_ref, second_ref, half_ref):
+    first, second = first_ref[...], second_ref[...]
+    even = lax.axis_index("fit") % 2 == 0
+    parts = [own_ref[...], near_ref[...], jnp.where(even, second, first), jnp.where(even, first, second)]
+    coefficients = jnp.concatenate(parts * 2, axis=0)
     half = jnp.dot(sums_ref[...], coefficients, preferred_element_type=jnp.float32)
     half_ref[...] = half.astype(jnp.bfloat16).reshape(half_ref.shape)
 
 
-def products(blocks, fits, *refs):
-    halves, keep_ref, send_ref, whole = refs[:blocks], refs[blocks], refs[blocks + 1], refs[blocks + 2]
+def shares():
+    senders = [{to: at for at, to in enumerate(r)} for r in ROUNDS]
+    table = []
+    for chip in range(16):
+        z, j = divmod(chip, 4)
+        if z == j:
+            table.append((3, 3, 0, 0))
+            continue
+        came = [divmod(s[chip], 4) for s in senders]
+        far = came.index((j, j))
+        (left,) = [q for p, q in came if p == z]
+        table.append((far, 3, came.index((j, left)), came.index((z, left))))
+    return table
+
+
+def products(one, two, three, own, keep_ref, send_ref, held):
     z, f = lax.axis_index("ao"), lax.axis_index("fit")
-    q, core = f // 2, f % 2
-    columns = keep_ref.shape[1]
-    for k in range(blocks):
-        total = None
-        for p in range(fits):
-            term = lax.dot_general(
-                halves[k][p], halves[0][p], (((1,), (1,)), ((), ())), preferred_element_type=jnp.float32
-            )
-            total = term if total is None else total + term
-        whole[k] = total
-    for k in range(blocks):
-        place = z ^ q ^ k
-        keep_ref[place] = whole[k, pl.ds(pl.multiple_of(core * columns, columns), columns), :]
-        send_ref[place] = whole[k, pl.ds(pl.multiple_of((1 - core) * columns, columns), columns), :]
+    chip, core = z * 4 + f // 2, f % 2
+    fits, block, _ = own.shape
+    columns = block // 2
+    for place, ref in enumerate((one, two, three, own)):
+        held[place] = jnp.concatenate([ref[p] for p in range(fits)], axis=1)
+
+    def place(n):
+        code = sum(row[n] << (2 * at) for at, row in enumerate(shares()))
+        return (jnp.int32(code - (1 << 32) if code >> 31 else code) >> (2 * chip)) & 3
+
+    def product(left, right):
+        return lax.dot_general(
+            left, right, (((1,), (1,)), ((), ())), preferred_element_type=jnp.float32
+        )
+
+    def put(total):
+        for side, whole in enumerate((total, total.T)):
+            for to, at in ((keep_ref, core), (send_ref, 1 - core)):
+                to[side] = jnp.where(at == 0, whole[:columns], whole[columns:])
+
+    first = product(held[place(0)], held[place(1)]) + product(held[place(2)], held[place(3)])
+
+    @pl.when(chip // 4 != chip % 4)
+    def _():
+        put(first)
+
+    @pl.when(chip // 4 == chip % 4)
+    def _():
+        put(first + product(held[1], held[1]) + product(held[2], held[2]))
 
 
 def permuted_form(blocks, coefficients, three_center, pair_blocks, pair_count):
@@ -117,10 +153,6 @@
     pairs = pair_blocks.shape[1]
     orbitals = coefficients.shape[1]
     columns = block // 2
-    chips = range(1, blocks)
-
-    def over_ao(x):
-        return [lax.ppermute(x, "ao", [(i, i ^ k) for i in range(blocks)]) for k in chips]
 
     def over_fit(x, k):
         return lax.ppermute(x, "fit", [(i, i ^ k) for i in range(2 * blocks)])
@@ -131,7 +163,14 @@
     def far(x):
         return pltpu.with_memory_space_constraint(x, pltpu.HBM)
 
-    coefs = [coefficients] + over_ao(coefficients)
+    def device(z, f):
+        return z * 2 * blocks + f
+
+    split = [
+        (device(z, f), device(z ^ (blocks - 1 - f % 2), f)) for z in range(blocks) for f in range(2 * blocks)
+    ]
+    first = lax.ppermute(coefficients, ("ao", "fit"), split)
+    near = lax.ppermute(coefficients, "ao", [(i, i ^ 1) for i in range(blocks)])
     sums = pl.pallas_call(
         functools.partial(slot_sums, blocks),
         out_shape=pltpu.VMEM((fits * block, 2 * blocks * block), jnp.bfloat16),
@@ -146,30 +185,44 @@
             pltpu.SMEM((blocks,), jnp.int32),
         ],
         compiler_params=pltpu.CompilerParams(vmem_limit_bytes=32 << 20),
+        cost_estimate=pl.CostEstimate(
+            flops=fits * block * wide, bytes_accessed=2 * fits * block * wide, transcendentals=0
+        ),
         name="slot_sums",
     )(far(pair_blocks), pair_count, far(three_center))
+    first, sums = lax.optimization_barrier((first, sums))
+    coefs = [coefficients, near, first, over_fit(first, 1)]
     half = pl.pallas_call(
-        functools.partial(transform, blocks),
+        transform,
         out_shape=pltpu.VMEM((fits, block, orbitals), jnp.bfloat16),
         in_specs=[VMEM] * (blocks + 1),
         out_specs=VMEM,
         name="transform",
     )(held(sums), *[held(x) for x in coefs])
-    halves = [half] + over_ao(half)
-    piece = pltpu.VMEM((blocks, columns, block), jnp.float32)
+    received = [
+        lax.ppermute(
+            half, ("ao", "fit"), [(2 * at + c, 2 * to + c) for at, to in enumerate(r) for c in range(2)]
+        )
+        for r in ROUNDS
+    ]
+    piece = pltpu.VMEM((2, columns, block), jnp.float32)
     keep, send = pl.pallas_call(
-        functools.partial(products, blocks, fits),
+        products,
         out_shape=(piece, piece),
-        in_specs=[VMEM] * blocks,
+        in_specs=[VMEM] * 4,
         out_specs=(VMEM, VMEM),
-        scratch_shapes=[pltpu.VMEM((blocks, block, block), jnp.float32)],
+        scratch_shapes=[pltpu.VMEM((4, block, fits * orbitals), jnp.bfloat16)],
         name="products",
-    )(*[held(x) for x in halves])
+    )(*[held(x) for x in received + [half]])
     chip = keep + over_fit(send, 1)
-    total = chip[0]
-    for k in chips:
-        total = total + over_fit(chip[k], 2 * k)
-    return total.T
+    across = [
+        (device(z, 2 * j + c), device(j, 2 * z + c))
+        for z in range(blocks)
+        for j in range(blocks)
+        for c in range(2)
+        if z != j
+    ]
+    return (chip[0] + lax.ppermute(chip[1], ("ao", "fit"), across)).T
 
 
 def solution(mesh):
@@ -179,8 +232,7 @@
         block = three_center.shape[1]
         fast = (
             fit == 2 * blocks
-            and blocks & (blocks - 1) == 0
-            and 1 < blocks <= 4
+            and blocks == 4
             and block % 128 == 0
             and coefficients.shape[1] % 128 == 0
             and coefficients.shape[0] == block

time: 33.6 us -> 31 us (0.923)
  the two profiles are of different devices: /device:TPU:0 before, /device:TPU:4 now
where the time goes in v3:
time: 31 us
  waiting for transfers between devices  14.9 us (48%)
  starting transfers between devices  11.1 us (36%)
  Pallas kernels  3.52 us (11%)
  between operations  0.73 us (2%)
  other arithmetic  0.63 us (2%)
    ppermute x3, waiting for transfers between devices, permuted_form(): lax.ppermute(half, ('ao', 'fit'), [(2 * at + c, 2 * to + c) for at, to in...  7.94 us
    ppermute x1, waiting for transfers between devices, permuted_form(): return (chip[0] + lax.ppermute(chip[1], ('ao', 'fit'), across)).T  4.55 us
    ppermute x3, starting transfers between devices, permuted_form(): lax.ppermute(half, ('ao', 'fit'), [(2 * at + c, 2 * to + c) for at, to in...  4.34 us
    ppermute x1, starting transfers between devices, permuted_form(): first = lax.ppermute(coefficients, ('ao', 'fit'), split)  3.6 us
    ppermute x1, starting transfers between devices, permuted_form(): return (chip[0] + lax.ppermute(chip[1], ('ao', 'fit'), across)).T  3.05 us
    pallas_call x1, Pallas kernels, permuted_form(): pl.pallas_call(functools.partial(slot_sums, blocks), out_shape=pltpu.VMEM...  2.74 us
    ppermute x2, waiting for transfers between devices, over_fit(): return lax.ppermute(x, 'fit', [(i, i ^ k) for i in range(2 * blocks)])  1.8 us
    ppermute x1, waiting for transfers between devices, permuted_form(): near = lax.ppermute(coefficients, 'ao', [(i, i ^ 1) for i in range(blocks)])  0.63 us
  transfers between devices with their start and end apart: 8, of which 6 were waited for; matrix products, arithmetic and copies ran while one was open for 0% of the time, Pallas kernels for 9%

profile of v3, /device:TPU:4, one launch (start us, length us, event | category | flops | bytes accessed | tf_op | source)
XLA Modules:
  0.0 31.0 jit_solution(2999584477883176582)
XLA Ops:
  0.0 0.0 copy-start
  0.0 3.6 %collective-permute-start = (bf16[128,128]{1,0:T(8,128)(2,1)}, bf16[128,128]{1,0:T(8,128)(2,1)S(1)}, u32[]{:S(2)}, u32[]{:S(2)}) collective-permute-start(bf16[128,128]{1,0:T(8,128)(2,1)} %own_ref.1), channel_id=1, source_target_pairs={{0,24},{1,17},{2,26},{3,19},{4,28},{5,21},{6,30},{7,23},{8,16},{9,... | collective-permute-start | bytes 98312 | tf_op jit(solution)/shard_map/ppermute | solution.py:172
  3.6 0.0 collective-permute-start.1
  4.3 2.7 %slot_sums.1.sums_ref = bf16[512,1024]{1,0:T(8,128)(2,1)S(1)} custom-call(s32[1,32]{1,0:T(1,128)} %pair_ref.1, s32[1]{0:T(128)S(6)} %copy.5.count_ref, bf16[4,128,4096]{2,1,0:T(8,128)(2,1)} %x_ref.1), custom_call_target="tpu_custom_call" | custom-call | flops 2097152 | bytes 4194304 | tf_op jit(solution)/shard_map/slot_sums/pallas_call | solution.py:174
  7.0 0.0 collective-permute-done.first_ref
  7.0 0.1 collective-permute-start.2
  7.1 0.6 %collective-permute-done.1.near_ref = bf16[128,128]{1,0:T(8,128)(2,1)S(1)} collective-permute-done((bf16[128,128]{1,0:T(8,128)(2,1)}, bf16[128,128]{1,0:T(8,128)(2,1)S(1)}, u32[]{:S(2)}, u32[]{:S(2)}) %collective-permute-start.1) | collective-permute-done | bytes 32800 | tf_op jit(solution)/shard_map/ppermute | solution.py:173
  7.7 0.6 %collective-permute-done.2.second_ref = bf16[128,128]{1,0:T(8,128)(2,1)S(1)} collective-permute-done((bf16[128,128]{1,0:T(8,128)(2,1)S(1)}, bf16[128,128]{1,0:T(8,128)(2,1)S(1)}, u32[]{:S(2)}, u32[]{:S(2)}) %collective-permute-start.2) | collective-permute-done | bytes 32800 | tf_op jit(solution)/shard_map/ppermute | solution.py:158
  8.3 0.0 copy-done
  8.3 0.4 %transform.1.own = bf16[4,128,128]{2,1,0:T(8,128)(2,1)S(1)} custom-call(bf16[512,1024]{1,0:T(8,128)(2,1)S(1)} %slot_sums.1.sums_ref, bf16[128,128]{1,0:T(8,128)(2,1)S(1)} %copy-done, bf16[128,128]{1,0:T(8,128)(2,1)S(1)} %collective-permute-done.1.near_ref, bf16[128,128]{1,0:T(8,128)(2,1)S(1)} %collective-permute-done.first_ref, ...), custom_call_target="tpu_custom_call" | custom-call | tf_op jit(solution)/shard_map/transform/pallas_call | solution.py:195
  8.7 2.4 %collective-permute-start.5 = (bf16[4,128,128]{2,1,0:T(8,128)(2,1)S(1)}, bf16[4,128,128]{2,1,0:T(8,128)(2,1)S(1)}, u32[]{:S(2)}, u32[]{:S(2)}) collective-permute-start(bf16[4,128,128]{2,1,0:T(8,128)(2,1)S(1)} %transform.1.own), channel_id=1, source_target_pairs={{0,16},{1,17},{2,4},{3,5},{4,24},{5,25},{6,0},{7,1},{8,14},{9,15},... | collective-permute-start | bytes 393224 | tf_op jit(solution)/shard_map/ppermute | solution.py:203
  11.2 1.7 %collective-permute-start.4 = (bf16[4,128,128]{2,1,0:T(8,128)(2,1)S(1)}, bf16[4,128,128]{2,1,0:T(8,128)(2,1)S(1)}, u32[]{:S(2)}, u32[]{:S(2)}) collective-permute-start(bf16[4,128,128]{2,1,0:T(8,128)(2,1)S(1)} %transform.1.own), channel_id=1, source_target_pairs={{0,24},{1,25},{2,0},{3,1},{4,8},{5,9},{6,16},{7,17},{8,18},{9,19},... | collective-permute-start | bytes 393224 | tf_op jit(solution)/shard_map/ppermute | solution.py:203
  12.9 0.2 collective-permute-start.3
  13.1 2.9 %collective-permute-done.5.three = bf16[4,128,128]{2,1,0:T(8,128)(2,1)S(1)} collective-permute-done((bf16[4,128,128]{2,1,0:T(8,128)(2,1)S(1)}, bf16[4,128,128]{2,1,0:T(8,128)(2,1)S(1)}, u32[]{:S(2)}, u32[]{:S(2)}) %collective-permute-start.5) | collective-permute-done | bytes 131104 | tf_op jit(solution)/shard_map/ppermute | solution.py:203
  16.0 5.0 %collective-permute-done.4.two = bf16[4,128,128]{2,1,0:T(8,128)(2,1)S(1)} collective-permute-done((bf16[4,128,128]{2,1,0:T(8,128)(2,1)S(1)}, bf16[4,128,128]{2,1,0:T(8,128)(2,1)S(1)}, u32[]{:S(2)}, u32[]{:S(2)}) %collective-permute-start.4) | collective-permute-done | bytes 131104 | tf_op jit(solution)/shard_map/ppermute | solution.py:203
  21.0 0.0 collective-permute-done.3.one
  21.0 0.3 %products.1 = (f32[2,64,128]{2,1,0:T(8,128)S(1)}, f32[2,64,128]{2,1,0:T(8,128)S(1)}) custom-call(bf16[4,128,128]{2,1,0:T(8,128)(2,1)S(1)} %collective-permute-done.3.one, bf16[4,128,128]{2,1,0:T(8,128)(2,1)S(1)} %collective-permute-done.4.two, bf16[4,128,128]{2,1,0:T(8,128)(2,1)S(1)} %collective-permute-done.5.three, bf16[4,128,128]{2,1,0:T(8,128)(2,1)S(1)} %transform.1.own), custom_call_target="tpu_custom_call" | custom-call | tf_op jit(solution)/shard_map/products/pallas_call | solution.py:209
  21.4 0.1 collective-permute-start.6
  21.5 1.2 %collective-permute-done.6 = f32[2,64,128]{2,1,0:T(8,128)S(1)} collective-permute-done((f32[2,64,128]{2,1,0:T(8,128)S(1)}, f32[2,64,128]{2,1,0:T(8,128)S(1)}, u32[]{:S(2)}, u32[]{:S(2)}) %collective-permute-start.6) | collective-permute-done | bytes 65568 | tf_op jit(solution)/shard_map/ppermute | solution.py:158
  22.7 3.0 %collective-permute-start.7 = (f32[64,128]{1,0:T(8,128)S(1)}, f32[64,128]{1,0:T(8,128)S(1)}, u32[]{:S(2)}, u32[]{:S(2)}) collective-permute-start(f32[64,128]{1,0:T(8,128)S(1)} %slice_bitcast_fusion), channel_id=1, source_target_pairs={{2,8},{3,9},{4,16},{5,17},{6,24},{7,25},{8,2},{9,3},{12,18},{13,19... | collective-permute-start | bytes 98312 | tf_op jit(solution)/shard_map/ppermute | solution.py:225
  25.8 4.6 %collective-permute-done.7 = f32[64,128]{1,0:T(8,128)S(1)} collective-permute-done((f32[64,128]{1,0:T(8,128)S(1)}, f32[64,128]{1,0:T(8,128)S(1)}, u32[]{:S(2)}, u32[]{:S(2)}) %collective-permute-start.7) | collective-permute-done | bytes 32800 | tf_op jit(solution)/shard_map/ppermute | solution.py:225
  30.3 0.6 %fusion.1 = f32[128,64]{0,1:T(8,128)} fusion(f32[64,128]{1,0:T(8,128)S(1)} %collective-permute-done.7, f32[2,64,128]{2,1,0:T(8,128)S(1)} %add.6), kind=kLoop, calls=%fused_computation.3 | loop fusion | flops 8192 | bytes 98304 | tf_op jit(solution)/shard_map/transpose | solution.py:225
  (2 shorter events, 0.0 us)
Async XLA Ops:
  0.0 8.3 %copy-start = (bf16[128,128]{1,0:T(8,128)(2,1)S(1)}, bf16[128,128]{1,0:T(8,128)(2,1)}, u32[]{:S(2)}) copy-start(bf16[128,128]{1,0:T(8,128)(2,1)} %own_ref.1) | copy-start | bytes 98308
  0.0 7.0 %collective-permute-start = (bf16[128,128]{1,0:T(8,128)(2,1)}, bf16[128,128]{1,0:T(8,128)(2,1)S(1)}, u32[]{:S(2)}, u32[]{:S(2)}) collective-permute-start(bf16[128,128]{1,0:T(8,128)(2,1)} %own_ref.1), channel_id=1, source_target_pairs={{0,24},{1,17},{2,26},{3,19},{4,28},{5,21},{6,30},{7,23},{8,16},{9,... | collective-permute-start | bytes 98312 | tf_op jit(solution)/shard_map/ppermute | solution.py:172
  3.6 4.1 %collective-permute-start.1 = (bf16[128,128]{1,0:T(8,128)(2,1)}, bf16[128,128]{1,0:T(8,128)(2,1)S(1)}, u32[]{:S(2)}, u32[]{:S(2)}) collective-permute-start(bf16[128,128]{1,0:T(8,128)(2,1)} %own_ref.1), channel_id=1, source_target_pairs={{0,8},{8,0},{16,24},{24,16},{1,9},{9,1},{17,25},{25,17},{2,10},{10... | collective-permute-start | bytes 98312 | tf_op jit(solution)/shard_map/ppermute | solution.py:173
  7.0 1.3 %collective-permute-start.2 = (bf16[128,128]{1,0:T(8,128)(2,1)S(1)}, bf16[128,128]{1,0:T(8,128)(2,1)S(1)}, u32[]{:S(2)}, u32[]{:S(2)}) collective-permute-start(bf16[128,128]{1,0:T(8,128)(2,1)S(1)} %collective-permute-done.first_ref), channel_id=1, source_target_pairs={{0,1},{1,0},{2,3},{3,2},{4,5},{5,4},{6,7},{7,6},{8,9},{9,8},{10,11... | collective-permute-start | bytes 98312 | tf_op jit(solution)/shard_map/ppermute | solution.py:158
  8.7 7.3 %collective-permute-start.5 = (bf16[4,128,128]{2,1,0:T(8,128)(2,1)S(1)}, bf16[4,128,128]{2,1,0:T(8,128)(2,1)S(1)}, u32[]{:S(2)}, u32[]{:S(2)}) collective-permute-start(bf16[4,128,128]{2,1,0:T(8,128)(2,1)S(1)} %transform.1.own), channel_id=1, source_target_pairs={{0,16},{1,17},{2,4},{3,5},{4,24},{5,25},{6,0},{7,1},{8,14},{9,15},... | collective-permute-start | bytes 393224 | tf_op jit(solution)/shard_map/ppermute | solution.py:203
  11.2 9.8 %collective-permute-start.4 = (bf16[4,128,128]{2,1,0:T(8,128)(2,1)S(1)}, bf16[4,128,128]{2,1,0:T(8,128)(2,1)S(1)}, u32[]{:S(2)}, u32[]{:S(2)}) collective-permute-start(bf16[4,128,128]{2,1,0:T(8,128)(2,1)S(1)} %transform.1.own), channel_id=1, source_target_pairs={{0,24},{1,25},{2,0},{3,1},{4,8},{5,9},{6,16},{7,17},{8,18},{9,19},... | collective-permute-start | bytes 393224 | tf_op jit(solution)/shard_map/ppermute | solution.py:203
  12.9 8.1 %collective-permute-start.3 = (bf16[4,128,128]{2,1,0:T(8,128)(2,1)S(1)}, bf16[4,128,128]{2,1,0:T(8,128)(2,1)S(1)}, u32[]{:S(2)}, u32[]{:S(2)}) collective-permute-start(bf16[4,128,128]{2,1,0:T(8,128)(2,1)S(1)} %transform.1.own), channel_id=1, source_target_pairs={{0,8},{1,9},{2,6},{3,7},{4,0},{5,1},{6,2},{7,3},{8,10},{9,11},{10,... | collective-permute-start | bytes 393224 | tf_op jit(solution)/shard_map/ppermute | solution.py:203
  21.4 1.3 %collective-permute-start.6 = (f32[2,64,128]{2,1,0:T(8,128)S(1)}, f32[2,64,128]{2,1,0:T(8,128)S(1)}, u32[]{:S(2)}, u32[]{:S(2)}) collective-permute-start(f32[2,64,128]{2,1,0:T(8,128)S(1)} %get-tuple-element.12), channel_id=1, source_target_pairs={{0,1},{1,0},{2,3},{3,2},{4,5},{5,4},{6,7},{7,6},{8,9},{9,8},{10,11... | collective-permute-start | bytes 196616 | tf_op jit(solution)/shard_map/ppermute | solution.py:158
  22.7 7.6 %collective-permute-start.7 = (f32[64,128]{1,0:T(8,128)S(1)}, f32[64,128]{1,0:T(8,128)S(1)}, u32[]{:S(2)}, u32[]{:S(2)}) collective-permute-start(f32[64,128]{1,0:T(8,128)S(1)} %slice_bitcast_fusion), channel_id=1, source_target_pairs={{2,8},{3,9},{4,16},{5,17},{6,24},{7,25},{8,2},{9,3},{12,18},{13,19... | collective-permute-start | bytes 98312 | tf_op jit(solution)/shard_map/ppermute | solution.py:225

commit v4 on v2

--- a/solution.py
+++ b/solution.py
@@ -11,6 +11,12 @@
 HBM = pl.BlockSpec(memory_space=pltpu.HBM)
 SMEM = pl.BlockSpec(memory_space=pltpu.SMEM)
 TOGETHER = 4
+REDUCE = (
+    (0, 1, 2, 6, 4, 5, 3, 7, 8, 12, 10, 11, 9, 13, 14, 15),
+    (1, 6, 0, 2, 7, 4, 5, 3, 10, 8, 11, 12, 15, 14, 13, 9),
+    (6, 2, 1, 0, 5, 3, 7, 4, 12, 11, 8, 10, 13, 15, 9, 14),
+    (2, 0, 6, 1, 3, 7, 4, 5, 11, 10, 12, 8, 14, 9, 15, 13),
+)
 
 
 def gathered_form(coefficients, three_center, pair_blocks, pair_count):
@@ -86,30 +92,42 @@
             sums_ref[rows, (blocks + place) * block : (blocks + place + 1) * block] = low
 
 
-def transform(blocks, sums_ref, *refs):
-    half_ref = refs[-1]
-    coefficients = jnp.concatenate([ref[...] for ref in refs[:-1]] * 2, axis=0)
+def transform(sums_ref, own_ref, third_ref, second_ref, near_ref, half_ref):
+    parts = [own_ref[...], near_ref[...], second_ref[...], third_ref[...]]
+    coefficients = jnp.concatenate(parts * 2, axis=0)
     half = jnp.dot(sums_ref[...], coefficients, preferred_element_type=jnp.float32)
     half_ref[...] = half.astype(jnp.bfloat16).reshape(half_ref.shape)
 
 
-def products(blocks, fits, *refs):
-    halves, keep_ref, send_ref, whole = refs[:blocks], refs[blocks], refs[blocks + 1], refs[blocks + 2]
+def blocks_sent():
+    codes = []
+    for targets in REDUCE:
+        code = 0
+        for chip, to in enumerate(targets):
+            z = chip // 4
+            code |= ((to % 4) ^ z if to // 4 == z else 3) << (2 * chip)
+        codes.append(code - (1 << 32) if code >> 31 else code)
+    return codes
+
+
+def products(near, own, far, keep_ref, send_ref, whole):
     z, f = lax.axis_index("ao"), lax.axis_index("fit")
-    q, core = f // 2, f % 2
+    chip, core = z * 4 + f // 2, f % 2
     columns = keep_ref.shape[1]
-    for k in range(blocks):
-        total = None
-        for p in range(fits):
-            term = lax.dot_general(
-                halves[k][p], halves[0][p], (((1,), (1,)), ((), ())), preferred_element_type=jnp.float32
-            )
-            total = term if total is None else total + term
-        whole[k] = total
-    for k in range(blocks):
-        place = z ^ q ^ k
-        keep_ref[place] = whole[k, pl.ds(pl.multiple_of(core * columns, columns), columns), :]
-        send_ref[place] = whole[k, pl.ds(pl.multiple_of((1 - core) * columns, columns), columns), :]
+
+    def rows(ref):
+        return jnp.concatenate([ref[p] for p in range(ref.shape[0])], axis=1)
+
+    mine, next_to, beyond = rows(own), rows(near), rows(far)
+    pairs = ((mine, mine), (next_to, mine), (beyond, mine), (beyond, next_to))
+    for n, (left, right) in enumerate(pairs):
+        whole[n] = lax.dot_general(
+            left, right, (((1,), (1,)), ((), ())), preferred_element_type=jnp.float32
+        )
+    for m, code in enumerate(blocks_sent()):
+        n = (jnp.int32(code) >> (2 * chip)) & 3
+        keep_ref[m] = whole[n, pl.ds(pl.multiple_of(core * columns, columns), columns), :]
+        send_ref[m] = whole[n, pl.ds(pl.multiple_of((1 - core) * columns, columns), columns), :]
 
 
 def permuted_form(blocks, coefficients, three_center, pair_blocks, pair_count):
@@ -117,10 +135,9 @@
     pairs = pair_blocks.shape[1]
     orbitals = coefficients.shape[1]
     columns = block // 2
-    chips = range(1, blocks)
-
-    def over_ao(x):
-        return [lax.ppermute(x, "ao", [(i, i ^ k) for i in range(blocks)]) for k in chips]
+
+    def over_ao(x, k):
+        return lax.ppermute(x, "ao", [(i, i ^ k) for i in range(blocks)])
 
     def over_fit(x, k):
         return lax.ppermute(x, "fit", [(i, i ^ k) for i in range(2 * blocks)])
@@ -131,7 +148,7 @@
     def far(x):
         return pltpu.with_memory_space_constraint(x, pltpu.HBM)
 
-    coefs = [coefficients] + over_ao(coefficients)
+    coefs = [over_ao(coefficients, k) for k in (3, 2, 1)]
     sums = pl.pallas_call(
         functools.partial(slot_sums, blocks),
         out_shape=pltpu.VMEM((fits * block, 2 * blocks * block), jnp.bfloat16),
@@ -146,29 +163,34 @@
             pltpu.SMEM((blocks,), jnp.int32),
         ],
         compiler_params=pltpu.CompilerParams(vmem_limit_bytes=32 << 20),
+        cost_estimate=pl.CostEstimate(
+            flops=fits * block * wide, bytes_accessed=2 * fits * block * wide, transcendentals=0
+        ),
         name="slot_sums",
     )(far(pair_blocks), pair_count, far(three_center))
     half = pl.pallas_call(
-        functools.partial(transform, blocks),
+        transform,
         out_shape=pltpu.VMEM((fits, block, orbitals), jnp.bfloat16),
         in_specs=[VMEM] * (blocks + 1),
         out_specs=VMEM,
         name="transform",
-    )(held(sums), *[held(x) for x in coefs])
-    halves = [half] + over_ao(half)
+    )(held(sums), *[held(x) for x in [coefficients] + coefs])
+    near, far_rows = over_ao(half, 1), over_ao(half, 2)
     piece = pltpu.VMEM((blocks, columns, block), jnp.float32)
     keep, send = pl.pallas_call(
-        functools.partial(products, blocks, fits),
+        products,
         out_shape=(piece, piece),
-        in_specs=[VMEM] * blocks,
+        in_specs=[VMEM] * 3,
         out_specs=(VMEM, VMEM),
         scratch_shapes=[pltpu.VMEM((blocks, block, block), jnp.float32)],
         name="products",
-    )(*[held(x) for x in halves])
+    )(held(near), held(half), held(far_rows))
     chip = keep + over_fit(send, 1)
-    total = chip[0]
-    for k in chips:
-        total = total + over_fit(chip[k], 2 * k)
+    total = None
+    for m, targets in enumerate(REDUCE):
+        pairs = [(2 * at + c, 2 * to + c) for at, to in enumerate(targets) for c in range(2)]
+        part = lax.ppermute(chip[m], ("ao", "fit"), pairs)
+        total = part if total is None else total + part
     return total.T
 
 
@@ -179,8 +201,7 @@
         block = three_center.shape[1]
         fast = (
             fit == 2 * blocks
-            and blocks & (blocks - 1) == 0
-            and 1 < blocks <= 4
+            and blocks == 4
             and block % 128 == 0
             and coefficients.shape[1] % 128 == 0
             and coefficients.shape[0] == block

time: 33.6 us -> 28.7 us (0.85)
  the two profiles are of different devices: /device:TPU:0 before, /device:TPU:6 now
where the time goes in v4:
time: 28.7 us; the launch traced here: 28.5 us
  starting transfers between devices  12.7 us (44%)
  waiting for transfers between devices  10.9 us (38%)
  Pallas kernels  3.49 us (12%)
  between operations  0.72 us (3%)
  other arithmetic  0.65 us (2%)
    ppermute x5, starting transfers between devices, over_ao(): return lax.ppermute(x, 'ao', [(i, i ^ k) for i in range(blocks)])  6.82 us
    ppermute x5, waiting for transfers between devices, over_ao(): return lax.ppermute(x, 'ao', [(i, i ^ k) for i in range(blocks)])  6.19 us
    ppermute x4, starting transfers between devices, permuted_form(): part = lax.ppermute(chip[m], ('ao', 'fit'), pairs)  5.84 us
    ppermute x4, waiting for transfers between devices, permuted_form(): part = lax.ppermute(chip[m], ('ao', 'fit'), pairs)  3.39 us
    pallas_call x1, Pallas kernels, permuted_form(): pl.pallas_call(functools.partial(slot_sums, blocks), out_shape=pltpu.VMEM...  2.74 us
    ppermute x1, waiting for transfers between devices, over_fit(): return lax.ppermute(x, 'fit', [(i, i ^ k) for i in range(2 * blocks)])  1.33 us
    transpose x1, other arithmetic, permuted_form(): return total.T  0.62 us
  transfers between devices with their start and end apart: 10, of which 7 were waited for; matrix products, arithmetic and copies ran while one was open for 0% of the time, Pallas kernels for 10%

profile of v4, /device:TPU:6, one launch (start us, length us, event | category | flops | bytes accessed | tf_op | source)
XLA Modules:
  0.0 28.5 jit_solution(14417561671537445730)
XLA Ops:
  0.0 0.0 copy-start
  0.0 2.6 %collective-permute-start.1 = (bf16[128,128]{1,0:T(8,128)(2,1)}, bf16[128,128]{1,0:T(8,128)(2,1)S(1)}, u32[]{:S(2)}, u32[]{:S(2)}) collective-permute-start(bf16[128,128]{1,0:T(8,128)(2,1)} %own_ref.1), channel_id=1, source_target_pairs={{0,16},{8,24},{16,0},{24,8},{1,17},{9,25},{17,1},{25,9},{2,18},{10... | collective-permute-start | bytes 98312 | tf_op jit(solution)/shard_map/ppermute | solution.py:140
  2.6 1.3 %collective-permute-start = (bf16[128,128]{1,0:T(8,128)(2,1)}, bf16[128,128]{1,0:T(8,128)(2,1)S(1)}, u32[]{:S(2)}, u32[]{:S(2)}) collective-permute-start(bf16[128,128]{1,0:T(8,128)(2,1)} %own_ref.1), channel_id=1, source_target_pairs={{0,24},{8,16},{16,8},{24,0},{1,25},{9,17},{17,9},{25,1},{2,26},{10... | collective-permute-start | bytes 98312 | tf_op jit(solution)/shard_map/ppermute | solution.py:140
  3.9 0.2 collective-permute-start.2
  4.8 2.7 %slot_sums.1.sums_ref = bf16[512,1024]{1,0:T(8,128)(2,1)S(1)} custom-call(s32[1,32]{1,0:T(1,128)} %pair_ref.1, s32[1]{0:T(128)S(6)} %copy.5.count_ref, bf16[4,128,4096]{2,1,0:T(8,128)(2,1)} %x_ref.1), custom_call_target="tpu_custom_call" | custom-call | flops 2097152 | bytes 4194304 | tf_op jit(solution)/shard_map/slot_sums/pallas_call | solution.py:152
  7.6 0.0 collective-permute-done.1.second_ref
  7.6 0.9 %collective-permute-done.third_ref = bf16[128,128]{1,0:T(8,128)(2,1)S(1)} collective-permute-done((bf16[128,128]{1,0:T(8,128)(2,1)}, bf16[128,128]{1,0:T(8,128)(2,1)S(1)}, u32[]{:S(2)}, u32[]{:S(2)}) %collective-permute-start) | collective-permute-done | bytes 32800 | tf_op jit(solution)/shard_map/ppermute | solution.py:140
  8.5 0.0 collective-permute-done.2.near_ref
  8.5 0.0 copy-done
  8.5 0.4 %transform.1.own = bf16[4,128,128]{2,1,0:T(8,128)(2,1)S(1)} custom-call(bf16[512,1024]{1,0:T(8,128)(2,1)S(1)} %slot_sums.1.sums_ref, bf16[128,128]{1,0:T(8,128)(2,1)S(1)} %copy-done, bf16[128,128]{1,0:T(8,128)(2,1)S(1)} %collective-permute-done.third_ref, bf16[128,128]{1,0:T(8,128)(2,1)S(1)} %collective-permute-done.1.second_ref, ...), custom_call_target="tpu_custom_call" | custom-call | tf_op jit(solution)/shard_map/transform/pallas_call | solution.py:171
  9.0 1.6 %collective-permute-start.4 = (bf16[4,128,128]{2,1,0:T(8,128)(2,1)S(1)}, bf16[4,128,128]{2,1,0:T(8,128)(2,1)S(1)}, u32[]{:S(2)}, u32[]{:S(2)}) collective-permute-start(bf16[4,128,128]{2,1,0:T(8,128)(2,1)S(1)} %transform.1.own), channel_id=1, source_target_pairs={{0,16},{8,24},{16,0},{24,8},{1,17},{9,25},{17,1},{25,9},{2,18},{10... | collective-permute-start | bytes 393224 | tf_op jit(solution)/shard_map/ppermute | solution.py:140
  10.6 1.0 %collective-permute-start.3 = (bf16[4,128,128]{2,1,0:T(8,128)(2,1)S(1)}, bf16[4,128,128]{2,1,0:T(8,128)(2,1)S(1)}, u32[]{:S(2)}, u32[]{:S(2)}) collective-permute-start(bf16[4,128,128]{2,1,0:T(8,128)(2,1)S(1)} %transform.1.own), channel_id=1, source_target_pairs={{0,8},{8,0},{16,24},{24,16},{1,9},{9,1},{17,25},{25,17},{2,10},{10... | collective-permute-start | bytes 393224 | tf_op jit(solution)/shard_map/ppermute | solution.py:140
  11.6 5.0 %collective-permute-done.4.far = bf16[4,128,128]{2,1,0:T(8,128)(2,1)S(1)} collective-permute-done((bf16[4,128,128]{2,1,0:T(8,128)(2,1)S(1)}, bf16[4,128,128]{2,1,0:T(8,128)(2,1)S(1)}, u32[]{:S(2)}, u32[]{:S(2)}) %collective-permute-start.4) | collective-permute-done | bytes 131104 | tf_op jit(solution)/shard_map/ppermute | solution.py:140
  16.6 0.2 collective-permute-done.3.near
  16.9 0.3 %products.1 = (f32[4,64,128]{2,1,0:T(8,128)S(1)}, f32[4,64,128]{2,1,0:T(8,128)S(1)}) custom-call(bf16[4,128,128]{2,1,0:T(8,128)(2,1)S(1)} %collective-permute-done.3.near, bf16[4,128,128]{2,1,0:T(8,128)(2,1)S(1)} %transform.1.own, bf16[4,128,128]{2,1,0:T(8,128)(2,1)S(1)} %collective-permute-done.4.far), custom_call_target="tpu_custom_call" | custom-call | tf_op jit(solution)/shard_map/products/pallas_call | solution.py:180
  17.2 0.1 collective-permute-start.5
  17.3 1.3 %collective-permute-done.5 = f32[4,64,128]{2,1,0:T(8,128)S(1)} collective-permute-done((f32[4,64,128]{2,1,0:T(8,128)S(1)}, f32[4,64,128]{2,1,0:T(8,128)S(1)}, u32[]{:S(2)}, u32[]{:S(2)}) %collective-permute-start.5) | collective-permute-done | bytes 131104 | tf_op jit(solution)/shard_map/ppermute | solution.py:143
  18.6 0.6 %collective-permute-start.7 = (f32[64,128]{1,0:T(8,128)S(1)}, f32[64,128]{1,0:T(8,128)S(1)}, u32[]{:S(2)}, u32[]{:S(2)}) collective-permute-start(f32[64,128]{1,0:T(8,128)S(1)} %get-tuple-element.9), channel_id=1, source_target_pairs={{0,2},{1,3},{2,12},{3,13},{4,0},{5,1},{6,4},{7,5},{8,14},{9,15},{1... | collective-permute-start | bytes 98312 | tf_op jit(solution)/shard_map/ppermute | solution.py:192
  19.2 1.9 %collective-permute-start.9 = (f32[64,128]{1,0:T(8,128)S(1)}, f32[64,128]{1,0:T(8,128)S(1)}, u32[]{:S(2)}, u32[]{:S(2)}) collective-permute-start(f32[64,128]{1,0:T(8,128)S(1)} %get-tuple-element.10), channel_id=1, source_target_pairs={{0,4},{1,5},{2,0},{3,1},{4,12},{5,13},{6,2},{7,3},{8,6},{9,7},{10,... | collective-permute-start | bytes 98312 | tf_op jit(solution)/shard_map/ppermute | solution.py:192
  21.1 0.1 collective-permute-start.8
  21.2 3.3 %collective-permute-start.6 = (f32[64,128]{1,0:T(8,128)S(1)}, f32[64,128]{1,0:T(8,128)S(1)}, u32[]{:S(2)}, u32[]{:S(2)}) collective-permute-start(f32[64,128]{1,0:T(8,128)S(1)} %get-tuple-element.12), channel_id=1, source_target_pairs={{0,0},{1,1},{2,2},{3,3},{4,4},{5,5},{6,12},{7,13},{8,8},{9,9},{10,... | collective-permute-start | bytes 98312 | tf_op jit(solution)/shard_map/ppermute | solution.py:192
  24.5 0.0 collective-permute-done.7
  24.5 0.4 %collective-permute-done.9 = f32[64,128]{1,0:T(8,128)S(1)} collective-permute-done((f32[64,128]{1,0:T(8,128)S(1)}, f32[64,128]{1,0:T(8,128)S(1)}, u32[]{:S(2)}, u32[]{:S(2)}) %collective-permute-start.9) | collective-permute-done | bytes 32800 | tf_op jit(solution)/shard_map/ppermute | solution.py:192
  24.9 1.0 %collective-permute-done.8 = f32[64,128]{1,0:T(8,128)S(1)} collective-permute-done((f32[64,128]{1,0:T(8,128)S(1)}, f32[64,128]{1,0:T(8,128)S(1)}, u32[]{:S(2)}, u32[]{:S(2)}) %collective-permute-start.8) | collective-permute-done | bytes 32800 | tf_op jit(solution)/shard_map/ppermute | solution.py:192
  25.9 2.0 %collective-permute-done.6 = f32[64,128]{1,0:T(8,128)S(1)} collective-permute-done((f32[64,128]{1,0:T(8,128)S(1)}, f32[64,128]{1,0:T(8,128)S(1)}, u32[]{:S(2)}, u32[]{:S(2)}) %collective-permute-start.6) | collective-permute-done | bytes 32800 | tf_op jit(solution)/shard_map/ppermute | solution.py:192
  27.9 0.6 %add_bitcast_fusion = f32[128,64]{0,1:T(8,128)} fusion(f32[64,128]{1,0:T(8,128)S(1)} %collective-permute-done.9, f32[64,128]{1,0:T(8,128)S(1)} %collective-permute-done.8, f32[64,128]{1,0:T(8,128)S(1)} %collective-permute-done.6, f32[64,128]{1,0:T(8,128)S(1)} %collective-permute-done.7), kind=kLoop, calls=%fused_computation.4 | loop fusion | flops 24576 | bytes 163840 | tf_op jit(solution)/shard_map/transpose | solution.py:194
  (2 shorter events, 0.0 us)
Async XLA Ops:
  0.0 8.5 %copy-start = (bf16[128,128]{1,0:T(8,128)(2,1)S(1)}, bf16[128,128]{1,0:T(8,128)(2,1)}, u32[]{:S(2)}) copy-start(bf16[128,128]{1,0:T(8,128)(2,1)} %own_ref.1) | copy-start | bytes 98308
  0.0 7.6 %collective-permute-start.1 = (bf16[128,128]{1,0:T(8,128)(2,1)}, bf16[128,128]{1,0:T(8,128)(2,1)S(1)}, u32[]{:S(2)}, u32[]{:S(2)}) collective-permute-start(bf16[128,128]{1,0:T(8,128)(2,1)} %own_ref.1), channel_id=1, source_target_pairs={{0,16},{8,24},{16,0},{24,8},{1,17},{9,25},{17,1},{25,9},{2,18},{10... | collective-permute-start | bytes 98312 | tf_op jit(solution)/shard_map/ppermute | solution.py:140
  2.6 5.9 %collective-permute-start = (bf16[128,128]{1,0:T(8,128)(2,1)}, bf16[128,128]{1,0:T(8,128)(2,1)S(1)}, u32[]{:S(2)}, u32[]{:S(2)}) collective-permute-start(bf16[128,128]{1,0:T(8,128)(2,1)} %own_ref.1), channel_id=1, source_target_pairs={{0,24},{8,16},{16,8},{24,0},{1,25},{9,17},{17,9},{25,1},{2,26},{10... | collective-permute-start | bytes 98312 | tf_op jit(solution)/shard_map/ppermute | solution.py:140
  3.9 4.6 %collective-permute-start.2 = (bf16[128,128]{1,0:T(8,128)(2,1)}, bf16[128,128]{1,0:T(8,128)(2,1)S(1)}, u32[]{:S(2)}, u32[]{:S(2)}) collective-permute-start(bf16[128,128]{1,0:T(8,128)(2,1)} %own_ref.1), channel_id=1, source_target_pairs={{0,8},{8,0},{16,24},{24,16},{1,9},{9,1},{17,25},{25,17},{2,10},{10... | collective-permute-start | bytes 98312 | tf_op jit(solution)/shard_map/ppermute | solution.py:140
  9.0 7.7 %collective-permute-start.4 = (bf16[4,128,128]{2,1,0:T(8,128)(2,1)S(1)}, bf16[4,128,128]{2,1,0:T(8,128)(2,1)S(1)}, u32[]{:S(2)}, u32[]{:S(2)}) collective-permute-start(bf16[4,128,128]{2,1,0:T(8,128)(2,1)S(1)} %transform.1.own), channel_id=1, source_target_pairs={{0,16},{8,24},{16,0},{24,8},{1,17},{9,25},{17,1},{25,9},{2,18},{10... | collective-permute-start | bytes 393224 | tf_op jit(solution)/shard_map/ppermute | solution.py:140
  10.6 6.3 %collective-permute-start.3 = (bf16[4,128,128]{2,1,0:T(8,128)(2,1)S(1)}, bf16[4,128,128]{2,1,0:T(8,128)(2,1)S(1)}, u32[]{:S(2)}, u32[]{:S(2)}) collective-permute-start(bf16[4,128,128]{2,1,0:T(8,128)(2,1)S(1)} %transform.1.own), channel_id=1, source_target_pairs={{0,8},{8,0},{16,24},{24,16},{1,9},{9,1},{17,25},{25,17},{2,10},{10... | collective-permute-start | bytes 393224 | tf_op jit(solution)/shard_map/ppermute | solution.py:140
  17.2 1.4 %collective-permute-start.5 = (f32[4,64,128]{2,1,0:T(8,128)S(1)}, f32[4,64,128]{2,1,0:T(8,128)S(1)}, u32[]{:S(2)}, u32[]{:S(2)}) collective-permute-start(f32[4,64,128]{2,1,0:T(8,128)S(1)} %get-tuple-element.8), channel_id=1, source_target_pairs={{0,1},{1,0},{2,3},{3,2},{4,5},{5,4},{6,7},{7,6},{8,9},{9,8},{10,11... | collective-permute-start | bytes 393224 | tf_op jit(solution)/shard_map/ppermute | solution.py:143
  18.6 5.9 %collective-permute-start.7 = (f32[64,128]{1,0:T(8,128)S(1)}, f32[64,128]{1,0:T(8,128)S(1)}, u32[]{:S(2)}, u32[]{:S(2)}) collective-permute-start(f32[64,128]{1,0:T(8,128)S(1)} %get-tuple-element.9), channel_id=1, source_target_pairs={{0,2},{1,3},{2,12},{3,13},{4,0},{5,1},{6,4},{7,5},{8,14},{9,15},{1... | collective-permute-start | bytes 98312 | tf_op jit(solution)/shard_map/ppermute | solution.py:192
  19.2 5.7 %collective-permute-start.9 = (f32[64,128]{1,0:T(8,128)S(1)}, f32[64,128]{1,0:T(8,128)S(1)}, u32[]{:S(2)}, u32[]{:S(2)}) collective-permute-start(f32[64,128]{1,0:T(8,128)S(1)} %get-tuple-element.10), channel_id=1, source_target_pairs={{0,4},{1,5},{2,0},{3,1},{4,12},{5,13},{6,2},{7,3},{8,6},{9,7},{10,... | collective-permute-start | bytes 98312 | tf_op jit(solution)/shard_map/ppermute | solution.py:192
  21.1 4.8 %collective-permute-start.8 = (f32[64,128]{1,0:T(8,128)S(1)}, f32[64,128]{1,0:T(8,128)S(1)}, u32[]{:S(2)}, u32[]{:S(2)}) collective-permute-start(f32[64,128]{1,0:T(8,128)S(1)} %get-tuple-element.11), channel_id=1, source_target_pairs={{0,12},{1,13},{2,4},{3,5},{4,2},{5,3},{6,0},{7,1},{8,10},{9,11},{1... | collective-permute-start | bytes 98312 | tf_op jit(solution)/shard_map/ppermute | solution.py:192
  21.2 6.7 %collective-permute-start.6 = (f32[64,128]{1,0:T(8,128)S(1)}, f32[64,128]{1,0:T(8,128)S(1)}, u32[]{:S(2)}, u32[]{:S(2)}) collective-permute-start(f32[64,128]{1,0:T(8,128)S(1)} %get-tuple-element.12), channel_id=1, source_target_pairs={{0,0},{1,1},{2,2},{3,3},{4,4},{5,5},{6,12},{7,13},{8,8},{9,9},{10,... | collective-permute-start | bytes 98312 | tf_op jit(solution)/shard_map/ppermute | solution.py:192

commit v5 on v4

--- a/solution.py
+++ b/solution.py
@@ -12,10 +12,10 @@
 SMEM = pl.BlockSpec(memory_space=pltpu.SMEM)
 TOGETHER = 4
 REDUCE = (
-    (0, 1, 2, 6, 4, 5, 3, 7, 8, 12, 10, 11, 9, 13, 14, 15),
-    (1, 6, 0, 2, 7, 4, 5, 3, 10, 8, 11, 12, 15, 14, 13, 9),
-    (6, 2, 1, 0, 5, 3, 7, 4, 12, 11, 8, 10, 13, 15, 9, 14),
-    (2, 0, 6, 1, 3, 7, 4, 5, 11, 10, 12, 8, 14, 9, 15, 13),
+    (0, 2, 6, 1, 4, 7, 3, 5, 12, 8, 10, 11, 13, 9, 15, 14),
+    (1, 0, 2, 6, 3, 5, 4, 7, 11, 10, 12, 8, 14, 13, 9, 15),
+    (6, 1, 0, 2, 5, 3, 7, 4, 10, 11, 8, 12, 15, 14, 13, 9),
+    (2, 6, 1, 0, 7, 4, 5, 3, 8, 12, 11, 10, 9, 15, 14, 13),
 )
 
 
@@ -126,8 +126,8 @@
         )
     for m, code in enumerate(blocks_sent()):
         n = (jnp.int32(code) >> (2 * chip)) & 3
-        keep_ref[m] = whole[n, pl.ds(pl.multiple_of(core * columns, columns), columns), :]
-        send_ref[m] = whole[n, pl.ds(pl.multiple_of((1 - core) * columns, columns), columns), :]
+        keep_ref[m] = whole[n, pl.ds(pl.multiple_of((1 - core) * columns, columns), columns), :]
+        send_ref[m] = whole[n, pl.ds(pl.multiple_of(core * columns, columns), columns), :]
 
 
 def permuted_form(blocks, coefficients, three_center, pair_blocks, pair_count):
@@ -188,7 +188,7 @@
     chip = keep + over_fit(send, 1)
     total = None
     for m, targets in enumerate(REDUCE):
-        pairs = [(2 * at + c, 2 * to + c) for at, to in enumerate(targets) for c in range(2)]
+        pairs = [(2 * at + c, 2 * to + 1 - c) for at, to in enumerate(targets) for c in range(2)]
         part = lax.ppermute(chip[m], ("ao", "fit"), pairs)
         total = part if total is None else total + part
     return total.T

time: 28.7 us -> 26.6 us (0.927)
  the two profiles are of different devices: /device:TPU:6 before, /device:TPU:0 now
where the time goes in v5:
time: 26.6 us; the launch traced here: 26.4 us
  starting transfers between devices  12 us (45%)
  waiting for transfers between devices  9.91 us (37%)
  Pallas kernels  3.12 us (12%)
  between operations  0.71 us (3%)
  other arithmetic  0.65 us (2%)
    ppermute x5, starting transfers between devices, over_ao(): return lax.ppermute(x, 'ao', [(i, i ^ k) for i in range(blocks)])  8.27 us
    ppermute x5, waiting for transfers between devices, over_ao(): return lax.ppermute(x, 'ao', [(i, i ^ k) for i in range(blocks)])  6.54 us
    ppermute x4, starting transfers between devices, permuted_form(): part = lax.ppermute(chip[m], ('ao', 'fit'), pairs)  3.62 us
    pallas_call x1, Pallas kernels, permuted_form(): pl.pallas_call(functools.partial(slot_sums, blocks), out_shape=pltpu.VMEM...  2.37 us
    ppermute x4, waiting for transfers between devices, permuted_form(): part = lax.ppermute(chip[m], ('ao', 'fit'), pairs)  2.03 us
    ppermute x1, waiting for transfers between devices, over_fit(): return lax.ppermute(x, 'fit', [(i, i ^ k) for i in range(2 * blocks)])  1.33 us
    transpose x1, other arithmetic, permuted_form(): return total.T  0.63 us
  transfers between devices with their start and end apart: 10, of which 5 were waited for; matrix products, arithmetic and copies ran while one was open for 0% of the time, Pallas kernels for 9%

profile of v5, /device:TPU:0, one launch (start us, length us, event | category | flops | bytes accessed | tf_op | source)
XLA Modules:
  0.0 26.4 jit_solution(13290109820769836787)
XLA Ops:
  0.0 0.0 copy-start
  0.0 4.0 %collective-permute-start.1 = (bf16[128,128]{1,0:T(8,128)(2,1)}, bf16[128,128]{1,0:T(8,128)(2,1)S(1)}, u32[]{:S(2)}, u32[]{:S(2)}) collective-permute-start(bf16[128,128]{1,0:T(8,128)(2,1)} %own_ref.1), channel_id=1, source_target_pairs={{0,16},{8,24},{16,0},{24,8},{1,17},{9,25},{17,1},{25,9},{2,18},{10... | collective-permute-start | bytes 98312 | tf_op jit(solution)/shard_map/ppermute | solution.py:140
  4.0 1.3 %collective-permute-start = (bf16[128,128]{1,0:T(8,128)(2,1)}, bf16[128,128]{1,0:T(8,128)(2,1)S(1)}, u32[]{:S(2)}, u32[]{:S(2)}) collective-permute-start(bf16[128,128]{1,0:T(8,128)(2,1)} %own_ref.1), channel_id=1, source_target_pairs={{0,24},{8,16},{16,8},{24,0},{1,25},{9,17},{17,9},{25,1},{2,26},{10... | collective-permute-start | bytes 98312 | tf_op jit(solution)/shard_map/ppermute | solution.py:140
  5.4 0.2 collective-permute-start.2
  6.3 2.4 %slot_sums.1.sums_ref = bf16[512,1024]{1,0:T(8,128)(2,1)S(1)} custom-call(s32[1,32]{1,0:T(1,128)} %pair_ref.1, s32[1]{0:T(128)S(6)} %copy.5.count_ref, bf16[4,128,4096]{2,1,0:T(8,128)(2,1)} %x_ref.1), custom_call_target="tpu_custom_call" | custom-call | flops 2097152 | bytes 4194304 | tf_op jit(solution)/shard_map/slot_sums/pallas_call | solution.py:152
  8.6 0.0 collective-permute-done.1.second_ref
  8.7 1.3 %collective-permute-done.third_ref = bf16[128,128]{1,0:T(8,128)(2,1)S(1)} collective-permute-done((bf16[128,128]{1,0:T(8,128)(2,1)}, bf16[128,128]{1,0:T(8,128)(2,1)S(1)}, u32[]{:S(2)}, u32[]{:S(2)}) %collective-permute-start) | collective-permute-done | bytes 32800 | tf_op jit(solution)/shard_map/ppermute | solution.py:140
  10.0 0.0 collective-permute-done.2.near_ref
  10.0 0.0 copy-done
  10.0 0.4 %transform.1.own = bf16[4,128,128]{2,1,0:T(8,128)(2,1)S(1)} custom-call(bf16[512,1024]{1,0:T(8,128)(2,1)S(1)} %slot_sums.1.sums_ref, bf16[128,128]{1,0:T(8,128)(2,1)S(1)} %copy-done, bf16[128,128]{1,0:T(8,128)(2,1)S(1)} %collective-permute-done.third_ref, bf16[128,128]{1,0:T(8,128)(2,1)S(1)} %collective-permute-done.1.second_ref, ...), custom_call_target="tpu_custom_call" | custom-call | tf_op jit(solution)/shard_map/transform/pallas_call | solution.py:171
  10.4 1.6 %collective-permute-start.4 = (bf16[4,128,128]{2,1,0:T(8,128)(2,1)S(1)}, bf16[4,128,128]{2,1,0:T(8,128)(2,1)S(1)}, u32[]{:S(2)}, u32[]{:S(2)}) collective-permute-start(bf16[4,128,128]{2,1,0:T(8,128)(2,1)S(1)} %transform.1.own), channel_id=1, source_target_pairs={{0,16},{8,24},{16,0},{24,8},{1,17},{9,25},{17,1},{25,9},{2,18},{10... | collective-permute-start | bytes 393224 | tf_op jit(solution)/shard_map/ppermute | solution.py:140
  12.0 1.1 %collective-permute-start.3 = (bf16[4,128,128]{2,1,0:T(8,128)(2,1)S(1)}, bf16[4,128,128]{2,1,0:T(8,128)(2,1)S(1)}, u32[]{:S(2)}, u32[]{:S(2)}) collective-permute-start(bf16[4,128,128]{2,1,0:T(8,128)(2,1)S(1)} %transform.1.own), channel_id=1, source_target_pairs={{0,8},{8,0},{16,24},{24,16},{1,9},{9,1},{17,25},{25,17},{2,10},{10... | collective-permute-start | bytes 393224 | tf_op jit(solution)/shard_map/ppermute | solution.py:140
  13.1 5.0 %collective-permute-done.4.far = bf16[4,128,128]{2,1,0:T(8,128)(2,1)S(1)} collective-permute-done((bf16[4,128,128]{2,1,0:T(8,128)(2,1)S(1)}, bf16[4,128,128]{2,1,0:T(8,128)(2,1)S(1)}, u32[]{:S(2)}, u32[]{:S(2)}) %collective-permute-start.4) | collective-permute-done | bytes 131104 | tf_op jit(solution)/shard_map/ppermute | solution.py:140
  18.1 0.2 collective-permute-done.3.near
  18.3 0.3 %products.1 = (f32[4,64,128]{2,1,0:T(8,128)S(1)}, f32[4,64,128]{2,1,0:T(8,128)S(1)}) custom-call(bf16[4,128,128]{2,1,0:T(8,128)(2,1)S(1)} %collective-permute-done.3.near, bf16[4,128,128]{2,1,0:T(8,128)(2,1)S(1)} %transform.1.own, bf16[4,128,128]{2,1,0:T(8,128)(2,1)S(1)} %collective-permute-done.4.far), custom_call_target="tpu_custom_call" | custom-call | tf_op jit(solution)/shard_map/products/pallas_call | solution.py:180
  18.6 0.1 collective-permute-start.5
  18.7 1.3 %collective-permute-done.5 = f32[4,64,128]{2,1,0:T(8,128)S(1)} collective-permute-done((f32[4,64,128]{2,1,0:T(8,128)S(1)}, f32[4,64,128]{2,1,0:T(8,128)S(1)}, u32[]{:S(2)}, u32[]{:S(2)}) %collective-permute-start.5) | collective-permute-done | bytes 131104 | tf_op jit(solution)/shard_map/ppermute | solution.py:143
  20.1 1.3 %collective-permute-start.7 = (f32[64,128]{1,0:T(8,128)S(1)}, f32[64,128]{1,0:T(8,128)S(1)}, u32[]{:S(2)}, u32[]{:S(2)}) collective-permute-start(f32[64,128]{1,0:T(8,128)S(1)} %get-tuple-element.9), channel_id=1, source_target_pairs={{0,3},{1,2},{2,1},{3,0},{4,5},{5,4},{6,13},{7,12},{8,7},{9,6},{10,... | collective-permute-start | bytes 98312 | tf_op jit(solution)/shard_map/ppermute | solution.py:192
  21.4 0.4 %collective-permute-start.9 = (f32[64,128]{1,0:T(8,128)S(1)}, f32[64,128]{1,0:T(8,128)S(1)}, u32[]{:S(2)}, u32[]{:S(2)}) collective-permute-start(f32[64,128]{1,0:T(8,128)S(1)} %get-tuple-element.10), channel_id=1, source_target_pairs={{0,5},{1,4},{2,13},{3,12},{4,3},{5,2},{6,1},{7,0},{8,15},{9,14},{1... | collective-permute-start | bytes 98312 | tf_op jit(solution)/shard_map/ppermute | solution.py:192
  21.8 1.6 %collective-permute-start.8 = (f32[64,128]{1,0:T(8,128)S(1)}, f32[64,128]{1,0:T(8,128)S(1)}, u32[]{:S(2)}, u32[]{:S(2)}) collective-permute-start(f32[64,128]{1,0:T(8,128)S(1)} %get-tuple-element.11), channel_id=1, source_target_pairs={{0,13},{1,12},{2,3},{3,2},{4,1},{5,0},{6,5},{7,4},{8,11},{9,10},{1... | collective-permute-start | bytes 98312 | tf_op jit(solution)/shard_map/ppermute | solution.py:192
  23.4 0.3 %collective-permute-start.6 = (f32[64,128]{1,0:T(8,128)S(1)}, f32[64,128]{1,0:T(8,128)S(1)}, u32[]{:S(2)}, u32[]{:S(2)}) collective-permute-start(f32[64,128]{1,0:T(8,128)S(1)} %get-tuple-element.12), channel_id=1, source_target_pairs={{0,1},{1,0},{2,5},{3,4},{4,13},{5,12},{6,3},{7,2},{8,9},{9,8},{10,... | collective-permute-start | bytes 98312 | tf_op jit(solution)/shard_map/ppermute | solution.py:192
  23.7 0.0 collective-permute-done.7
  23.7 2.0 %collective-permute-done.9 = f32[64,128]{1,0:T(8,128)S(1)} collective-permute-done((f32[64,128]{1,0:T(8,128)S(1)}, f32[64,128]{1,0:T(8,128)S(1)}, u32[]{:S(2)}, u32[]{:S(2)}) %collective-permute-start.9) | collective-permute-done | bytes 32800 | tf_op jit(solution)/shard_map/ppermute | solution.py:192
  25.7 0.0 collective-permute-done.8
  25.7 0.0 collective-permute-done.6
  25.7 0.6 %add_bitcast_fusion = f32[128,64]{0,1:T(8,128)} fusion(f32[64,128]{1,0:T(8,128)S(1)} %collective-permute-done.9, f32[64,128]{1,0:T(8,128)S(1)} %collective-permute-done.8, f32[64,128]{1,0:T(8,128)S(1)} %collective-permute-done.6, f32[64,128]{1,0:T(8,128)S(1)} %collective-permute-done.7), kind=kLoop, calls=%fused_computation.4 | loop fusion | flops 24576 | bytes 163840 | tf_op jit(solution)/shard_map/transpose | solution.py:194
  (2 shorter events, 0.0 us)
Async XLA Ops:
  0.0 10.0 %copy-start = (bf16[128,128]{1,0:T(8,128)(2,1)S(1)}, bf16[128,128]{1,0:T(8,128)(2,1)}, u32[]{:S(2)}) copy-start(bf16[128,128]{1,0:T(8,128)(2,1)} %own_ref.1) | copy-start | bytes 98308
  0.0 8.6 %collective-permute-start.1 = (bf16[128,128]{1,0:T(8,128)(2,1)}, bf16[128,128]{1,0:T(8,128)(2,1)S(1)}, u32[]{:S(2)}, u32[]{:S(2)}) collective-permute-start(bf16[128,128]{1,0:T(8,128)(2,1)} %own_ref.1), channel_id=1, source_target_pairs={{0,16},{8,24},{16,0},{24,8},{1,17},{9,25},{17,1},{25,9},{2,18},{10... | collective-permute-start | bytes 98312 | tf_op jit(solution)/shard_map/ppermute | solution.py:140
  4.0 5.9 %collective-permute-start = (bf16[128,128]{1,0:T(8,128)(2,1)}, bf16[128,128]{1,0:T(8,128)(2,1)S(1)}, u32[]{:S(2)}, u32[]{:S(2)}) collective-permute-start(bf16[128,128]{1,0:T(8,128)(2,1)} %own_ref.1), channel_id=1, source_target_pairs={{0,24},{8,16},{16,8},{24,0},{1,25},{9,17},{17,9},{25,1},{2,26},{10... | collective-permute-start | bytes 98312 | tf_op jit(solution)/shard_map/ppermute | solution.py:140
  5.4 4.6 %collective-permute-start.2 = (bf16[128,128]{1,0:T(8,128)(2,1)}, bf16[128,128]{1,0:T(8,128)(2,1)S(1)}, u32[]{:S(2)}, u32[]{:S(2)}) collective-permute-start(bf16[128,128]{1,0:T(8,128)(2,1)} %own_ref.1), channel_id=1, source_target_pairs={{0,8},{8,0},{16,24},{24,16},{1,9},{9,1},{17,25},{25,17},{2,10},{10... | collective-permute-start | bytes 98312 | tf_op jit(solution)/shard_map/ppermute | solution.py:140
  10.4 7.7 %collective-permute-start.4 = (bf16[4,128,128]{2,1,0:T(8,128)(2,1)S(1)}, bf16[4,128,128]{2,1,0:T(8,128)(2,1)S(1)}, u32[]{:S(2)}, u32[]{:S(2)}) collective-permute-start(bf16[4,128,128]{2,1,0:T(8,128)(2,1)S(1)} %transform.1.own), channel_id=1, source_target_pairs={{0,16},{8,24},{16,0},{24,8},{1,17},{9,25},{17,1},{25,9},{2,18},{10... | collective-permute-start | bytes 393224 | tf_op jit(solution)/shard_map/ppermute | solution.py:140
  12.0 6.3 %collective-permute-start.3 = (bf16[4,128,128]{2,1,0:T(8,128)(2,1)S(1)}, bf16[4,128,128]{2,1,0:T(8,128)(2,1)S(1)}, u32[]{:S(2)}, u32[]{:S(2)}) collective-permute-start(bf16[4,128,128]{2,1,0:T(8,128)(2,1)S(1)} %transform.1.own), channel_id=1, source_target_pairs={{0,8},{8,0},{16,24},{24,16},{1,9},{9,1},{17,25},{25,17},{2,10},{10... | collective-permute-start | bytes 393224 | tf_op jit(solution)/shard_map/ppermute | solution.py:140
  18.6 1.4 %collective-permute-start.5 = (f32[4,64,128]{2,1,0:T(8,128)S(1)}, f32[4,64,128]{2,1,0:T(8,128)S(1)}, u32[]{:S(2)}, u32[]{:S(2)}) collective-permute-start(f32[4,64,128]{2,1,0:T(8,128)S(1)} %get-tuple-element.8), channel_id=1, source_target_pairs={{0,1},{1,0},{2,3},{3,2},{4,5},{5,4},{6,7},{7,6},{8,9},{9,8},{10,11... | collective-permute-start | bytes 393224 | tf_op jit(solution)/shard_map/ppermute | solution.py:143
  20.1 3.6 %collective-permute-start.7 = (f32[64,128]{1,0:T(8,128)S(1)}, f32[64,128]{1,0:T(8,128)S(1)}, u32[]{:S(2)}, u32[]{:S(2)}) collective-permute-start(f32[64,128]{1,0:T(8,128)S(1)} %get-tuple-element.9), channel_id=1, source_target_pairs={{0,3},{1,2},{2,1},{3,0},{4,5},{5,4},{6,13},{7,12},{8,7},{9,6},{10,... | collective-permute-start | bytes 98312 | tf_op jit(solution)/shard_map/ppermute | solution.py:192
  21.4 4.4 %collective-permute-start.9 = (f32[64,128]{1,0:T(8,128)S(1)}, f32[64,128]{1,0:T(8,128)S(1)}, u32[]{:S(2)}, u32[]{:S(2)}) collective-permute-start(f32[64,128]{1,0:T(8,128)S(1)} %get-tuple-element.10), channel_id=1, source_target_pairs={{0,5},{1,4},{2,13},{3,12},{4,3},{5,2},{6,1},{7,0},{8,15},{9,14},{1... | collective-permute-start | bytes 98312 | tf_op jit(solution)/shard_map/ppermute | solution.py:192
  21.8 4.0 %collective-permute-start.8 = (f32[64,128]{1,0:T(8,128)S(1)}, f32[64,128]{1,0:T(8,128)S(1)}, u32[]{:S(2)}, u32[]{:S(2)}) collective-permute-start(f32[64,128]{1,0:T(8,128)S(1)} %get-tuple-element.11), channel_id=1, source_target_pairs={{0,13},{1,12},{2,3},{3,2},{4,1},{5,0},{6,5},{7,4},{8,11},{9,10},{1... | collective-permute-start | bytes 98312 | tf_op jit(solution)/shard_map/ppermute | solution.py:192
  23.4 2.4 %collective-permute-start.6 = (f32[64,128]{1,0:T(8,128)S(1)}, f32[64,128]{1,0:T(8,128)S(1)}, u32[]{:S(2)}, u32[]{:S(2)}) collective-permute-start(f32[64,128]{1,0:T(8,128)S(1)} %get-tuple-element.12), channel_id=1, source_target_pairs={{0,1},{1,0},{2,5},{3,4},{4,13},{5,12},{6,3},{7,2},{8,9},{9,8},{10,... | collective-permute-start | bytes 98312 | tf_op jit(solution)/shard_map/ppermute | solution.py:192

commit v6 on v5

--- a/solution.py
+++ b/solution.py
@@ -110,7 +110,7 @@
     return codes
 
 
-def products(near, own, far, keep_ref, send_ref, whole):
+def products(near, far, own, keep_ref, send_ref, whole):
     z, f = lax.axis_index("ao"), lax.axis_index("fit")
     chip, core = z * 4 + f // 2, f % 2
     columns = keep_ref.shape[1]
@@ -184,7 +184,7 @@
         out_specs=(VMEM, VMEM),
         scratch_shapes=[pltpu.VMEM((blocks, block, block), jnp.float32)],
         name="products",
-    )(held(near), held(half), held(far_rows))
+    )(held(near), held(far_rows), held(half))
     chip = keep + over_fit(send, 1)
     total = None
     for m, targets in enumerate(REDUCE):

time: 26.6 us -> 26.6 us (level)
  waiting for transfers between devices: 9.91 us -> 9.59 us
  Pallas kernels: 3.12 us -> 3.39 us
    ppermute x5, waiting for transfers between devices: 6.54 us -> 6.26 us  [over_ao(): return lax.ppermute(x, 'ao', [(i, i ^ k) for i in range(blocks)])]
    pallas_call x1, Pallas kernels: 2.37 us -> 2.64 us  [permuted_form(): pl.pallas_call(functools.partial(slot_sums, blocks), out_shape=pltpu.VMEM...]
  transfers between devices with their start and end apart: 10 -> 10, of which waited for: 5 -> 5; matrix products, arithmetic and copies ran while one was open for 0% -> 0% of each run, Pallas kernels for 9% -> 10%
where the time goes in v6:
time: 26.6 us; the launch traced here: 26.3 us
  starting transfers between devices  12 us (45%)
  waiting for transfers between devices  9.59 us (36%)
  Pallas kernels  3.39 us (13%)
  between operations  0.71 us (3%)
  other arithmetic  0.65 us (2%)
    ppermute x5, starting transfers between devices, over_ao(): return lax.ppermute(x, 'ao', [(i, i ^ k) for i in range(blocks)])  8.27 us
    ppermute x5, waiting for transfers between devices, over_ao(): return lax.ppermute(x, 'ao', [(i, i ^ k) for i in range(blocks)])  6.26 us
    ppermute x4, starting transfers between devices, permuted_form(): part = lax.ppermute(chip[m], ('ao', 'fit'), pairs)  3.67 us
    pallas_call x1, Pallas kernels, permuted_form(): pl.pallas_call(functools.partial(slot_sums, blocks), out_shape=pltpu.VMEM...  2.64 us
    ppermute x4, waiting for transfers between devices, permuted_form(): part = lax.ppermute(chip[m], ('ao', 'fit'), pairs)  1.99 us
    ppermute x1, waiting for transfers between devices, over_fit(): return lax.ppermute(x, 'fit', [(i, i ^ k) for i in range(2 * blocks)])  1.33 us
    transpose x1, other arithmetic, permuted_form(): return total.T  0.63 us
  transfers between devices with their start and end apart: 10, of which 5 were waited for; matrix products, arithmetic and copies ran while one was open for 0% of the time, Pallas kernels for 10%

profile of v6, /device:TPU:0, one launch (start us, length us, event | category | flops | bytes accessed | tf_op | source)
XLA Modules:
  0.0 26.3 jit_solution(13100800610003576863)
XLA Ops:
  0.0 0.0 copy-start
  0.0 4.0 %collective-permute-start.1 = (bf16[128,128]{1,0:T(8,128)(2,1)}, bf16[128,128]{1,0:T(8,128)(2,1)S(1)}, u32[]{:S(2)}, u32[]{:S(2)}) collective-permute-start(bf16[128,128]{1,0:T(8,128)(2,1)} %own_ref.1), channel_id=1, source_target_pairs={{0,16},{8,24},{16,0},{24,8},{1,17},{9,25},{17,1},{25,9},{2,18},{10... | collective-permute-start | bytes 98312 | tf_op jit(solution)/shard_map/ppermute | solution.py:140
  4.0 1.3 %collective-permute-start = (bf16[128,128]{1,0:T(8,128)(2,1)}, bf16[128,128]{1,0:T(8,128)(2,1)S(1)}, u32[]{:S(2)}, u32[]{:S(2)}) collective-permute-start(bf16[128,128]{1,0:T(8,128)(2,1)} %own_ref.1), channel_id=1, source_target_pairs={{0,24},{8,16},{16,8},{24,0},{1,25},{9,17},{17,9},{25,1},{2,26},{10... | collective-permute-start | bytes 98312 | tf_op jit(solution)/shard_map/ppermute | solution.py:140
  5.4 0.2 collective-permute-start.2
  6.3 2.6 %slot_sums.1.sums_ref = bf16[512,1024]{1,0:T(8,128)(2,1)S(1)} custom-call(s32[1,32]{1,0:T(1,128)} %pair_ref.1, s32[1]{0:T(128)S(6)} %copy.5.count_ref, bf16[4,128,4096]{2,1,0:T(8,128)(2,1)} %x_ref.1), custom_call_target="tpu_custom_call" | custom-call | flops 2097152 | bytes 4194304 | tf_op jit(solution)/shard_map/slot_sums/pallas_call | solution.py:152
  8.9 0.0 collective-permute-done.1.second_ref
  8.9 1.0 %collective-permute-done.third_ref = bf16[128,128]{1,0:T(8,128)(2,1)S(1)} collective-permute-done((bf16[128,128]{1,0:T(8,128)(2,1)}, bf16[128,128]{1,0:T(8,128)(2,1)S(1)}, u32[]{:S(2)}, u32[]{:S(2)}) %collective-permute-start) | collective-permute-done | bytes 32800 | tf_op jit(solution)/shard_map/ppermute | solution.py:140
  10.0 0.0 collective-permute-done.2.near_ref
  10.0 0.0 copy-done
  10.0 0.4 %transform.1.own = bf16[4,128,128]{2,1,0:T(8,128)(2,1)S(1)} custom-call(bf16[512,1024]{1,0:T(8,128)(2,1)S(1)} %slot_sums.1.sums_ref, bf16[128,128]{1,0:T(8,128)(2,1)S(1)} %copy-done, bf16[128,128]{1,0:T(8,128)(2,1)S(1)} %collective-permute-done.third_ref, bf16[128,128]{1,0:T(8,128)(2,1)S(1)} %collective-permute-done.1.second_ref, ...), custom_call_target="tpu_custom_call" | custom-call | tf_op jit(solution)/shard_map/transform/pallas_call | solution.py:171
  10.4 1.6 %collective-permute-start.4 = (bf16[4,128,128]{2,1,0:T(8,128)(2,1)S(1)}, bf16[4,128,128]{2,1,0:T(8,128)(2,1)S(1)}, u32[]{:S(2)}, u32[]{:S(2)}) collective-permute-start(bf16[4,128,128]{2,1,0:T(8,128)(2,1)S(1)} %transform.1.own), channel_id=1, source_target_pairs={{0,16},{8,24},{16,0},{24,8},{1,17},{9,25},{17,1},{25,9},{2,18},{10... | collective-permute-start | bytes 393224 | tf_op jit(solution)/shard_map/ppermute | solution.py:140
  12.0 1.0 %collective-permute-start.3 = (bf16[4,128,128]{2,1,0:T(8,128)(2,1)S(1)}, bf16[4,128,128]{2,1,0:T(8,128)(2,1)S(1)}, u32[]{:S(2)}, u32[]{:S(2)}) collective-permute-start(bf16[4,128,128]{2,1,0:T(8,128)(2,1)S(1)} %transform.1.own), channel_id=1, source_target_pairs={{0,8},{8,0},{16,24},{24,16},{1,9},{9,1},{17,25},{25,17},{2,10},{10... | collective-permute-start | bytes 393224 | tf_op jit(solution)/shard_map/ppermute | solution.py:140
  13.1 5.0 %collective-permute-done.4.far = bf16[4,128,128]{2,1,0:T(8,128)(2,1)S(1)} collective-permute-done((bf16[4,128,128]{2,1,0:T(8,128)(2,1)S(1)}, bf16[4,128,128]{2,1,0:T(8,128)(2,1)S(1)}, u32[]{:S(2)}, u32[]{:S(2)}) %collective-permute-start.4) | collective-permute-done | bytes 131104 | tf_op jit(solution)/shard_map/ppermute | solution.py:140
  18.1 0.2 collective-permute-done.3.near
  18.3 0.3 %products.1 = (f32[4,64,128]{2,1,0:T(8,128)S(1)}, f32[4,64,128]{2,1,0:T(8,128)S(1)}) custom-call(bf16[4,128,128]{2,1,0:T(8,128)(2,1)S(1)} %collective-permute-done.3.near, bf16[4,128,128]{2,1,0:T(8,128)(2,1)S(1)} %collective-permute-done.4.far, bf16[4,128,128]{2,1,0:T(8,128)(2,1)S(1)} %transform.1.own), custom_call_target="tpu_custom_call" | custom-call | tf_op jit(solution)/shard_map/products/pallas_call | solution.py:180
  18.6 0.1 collective-permute-start.5
  18.7 1.3 %collective-permute-done.5 = f32[4,64,128]{2,1,0:T(8,128)S(1)} collective-permute-done((f32[4,64,128]{2,1,0:T(8,128)S(1)}, f32[4,64,128]{2,1,0:T(8,128)S(1)}, u32[]{:S(2)}, u32[]{:S(2)}) %collective-permute-start.5) | collective-permute-done | bytes 131104 | tf_op jit(solution)/shard_map/ppermute | solution.py:143
  20.1 1.3 %collective-permute-start.7 = (f32[64,128]{1,0:T(8,128)S(1)}, f32[64,128]{1,0:T(8,128)S(1)}, u32[]{:S(2)}, u32[]{:S(2)}) collective-permute-start(f32[64,128]{1,0:T(8,128)S(1)} %get-tuple-element.9), channel_id=1, source_target_pairs={{0,3},{1,2},{2,1},{3,0},{4,5},{5,4},{6,13},{7,12},{8,7},{9,6},{10,... | collective-permute-start | bytes 98312 | tf_op jit(solution)/shard_map/ppermute | solution.py:192
  21.4 0.4 %collective-permute-start.9 = (f32[64,128]{1,0:T(8,128)S(1)}, f32[64,128]{1,0:T(8,128)S(1)}, u32[]{:S(2)}, u32[]{:S(2)}) collective-permute-start(f32[64,128]{1,0:T(8,128)S(1)} %get-tuple-element.10), channel_id=1, source_target_pairs={{0,5},{1,4},{2,13},{3,12},{4,3},{5,2},{6,1},{7,0},{8,15},{9,14},{1... | collective-permute-start | bytes 98312 | tf_op jit(solution)/shard_map/ppermute | solution.py:192
  21.7 1.6 %collective-permute-start.8 = (f32[64,128]{1,0:T(8,128)S(1)}, f32[64,128]{1,0:T(8,128)S(1)}, u32[]{:S(2)}, u32[]{:S(2)}) collective-permute-start(f32[64,128]{1,0:T(8,128)S(1)} %get-tuple-element.11), channel_id=1, source_target_pairs={{0,13},{1,12},{2,3},{3,2},{4,1},{5,0},{6,5},{7,4},{8,11},{9,10},{1... | collective-permute-start | bytes 98312 | tf_op jit(solution)/shard_map/ppermute | solution.py:192
  23.4 0.3 %collective-permute-start.6 = (f32[64,128]{1,0:T(8,128)S(1)}, f32[64,128]{1,0:T(8,128)S(1)}, u32[]{:S(2)}, u32[]{:S(2)}) collective-permute-start(f32[64,128]{1,0:T(8,128)S(1)} %get-tuple-element.12), channel_id=1, source_target_pairs={{0,1},{1,0},{2,5},{3,4},{4,13},{5,12},{6,3},{7,2},{8,9},{9,8},{10,... | collective-permute-start | bytes 98312 | tf_op jit(solution)/shard_map/ppermute | solution.py:192
  23.7 0.0 collective-permute-done.7
  23.7 2.0 %collective-permute-done.9 = f32[64,128]{1,0:T(8,128)S(1)} collective-permute-done((f32[64,128]{1,0:T(8,128)S(1)}, f32[64,128]{1,0:T(8,128)S(1)}, u32[]{:S(2)}, u32[]{:S(2)}) %collective-permute-start.9) | collective-permute-done | bytes 32800 | tf_op jit(solution)/shard_map/ppermute | solution.py:192
  25.7 0.0 collective-permute-done.8
  25.7 0.0 collective-permute-done.6
  25.7 0.6 %add_bitcast_fusion = f32[128,64]{0,1:T(8,128)} fusion(f32[64,128]{1,0:T(8,128)S(1)} %collective-permute-done.9, f32[64,128]{1,0:T(8,128)S(1)} %collective-permute-done.8, f32[64,128]{1,0:T(8,128)S(1)} %collective-permute-done.6, f32[64,128]{1,0:T(8,128)S(1)} %collective-permute-done.7), kind=kLoop, calls=%fused_computation.4 | loop fusion | flops 24576 | bytes 163840 | tf_op jit(solution)/shard_map/transpose | solution.py:194
  (2 shorter events, 0.0 us)
Async XLA Ops:
  0.0 10.0 %copy-start = (bf16[128,128]{1,0:T(8,128)(2,1)S(1)}, bf16[128,128]{1,0:T(8,128)(2,1)}, u32[]{:S(2)}) copy-start(bf16[128,128]{1,0:T(8,128)(2,1)} %own_ref.1) | copy-start | bytes 98308
  0.0 8.9 %collective-permute-start.1 = (bf16[128,128]{1,0:T(8,128)(2,1)}, bf16[128,128]{1,0:T(8,128)(2,1)S(1)}, u32[]{:S(2)}, u32[]{:S(2)}) collective-permute-start(bf16[128,128]{1,0:T(8,128)(2,1)} %own_ref.1), channel_id=1, source_target_pairs={{0,16},{8,24},{16,0},{24,8},{1,17},{9,25},{17,1},{25,9},{2,18},{10... | collective-permute-start | bytes 98312 | tf_op jit(solution)/shard_map/ppermute | solution.py:140
  4.0 5.9 %collective-permute-start = (bf16[128,128]{1,0:T(8,128)(2,1)}, bf16[128,128]{1,0:T(8,128)(2,1)S(1)}, u32[]{:S(2)}, u32[]{:S(2)}) collective-permute-start(bf16[128,128]{1,0:T(8,128)(2,1)} %own_ref.1), channel_id=1, source_target_pairs={{0,24},{8,16},{16,8},{24,0},{1,25},{9,17},{17,9},{25,1},{2,26},{10... | collective-permute-start | bytes 98312 | tf_op jit(solution)/shard_map/ppermute | solution.py:140
  5.4 4.6 %collective-permute-start.2 = (bf16[128,128]{1,0:T(8,128)(2,1)}, bf16[128,128]{1,0:T(8,128)(2,1)S(1)}, u32[]{:S(2)}, u32[]{:S(2)}) collective-permute-start(bf16[128,128]{1,0:T(8,128)(2,1)} %own_ref.1), channel_id=1, source_target_pairs={{0,8},{8,0},{16,24},{24,16},{1,9},{9,1},{17,25},{25,17},{2,10},{10... | collective-permute-start | bytes 98312 | tf_op jit(solution)/shard_map/ppermute | solution.py:140
  10.4 7.7 %collective-permute-start.4 = (bf16[4,128,128]{2,1,0:T(8,128)(2,1)S(1)}, bf16[4,128,128]{2,1,0:T(8,128)(2,1)S(1)}, u32[]{:S(2)}, u32[]{:S(2)}) collective-permute-start(bf16[4,128,128]{2,1,0:T(8,128)(2,1)S(1)} %transform.1.own), channel_id=1, source_target_pairs={{0,16},{8,24},{16,0},{24,8},{1,17},{9,25},{17,1},{25,9},{2,18},{10... | collective-permute-start | bytes 393224 | tf_op jit(solution)/shard_map/ppermute | solution.py:140
  12.0 6.3 %collective-permute-start.3 = (bf16[4,128,128]{2,1,0:T(8,128)(2,1)S(1)}, bf16[4,128,128]{2,1,0:T(8,128)(2,1)S(1)}, u32[]{:S(2)}, u32[]{:S(2)}) collective-permute-start(bf16[4,128,128]{2,1,0:T(8,128)(2,1)S(1)} %transform.1.own), channel_id=1, source_target_pairs={{0,8},{8,0},{16,24},{24,16},{1,9},{9,1},{17,25},{25,17},{2,10},{10... | collective-permute-start | bytes 393224 | tf_op jit(solution)/shard_map/ppermute | solution.py:140
  18.6 1.4 %collective-permute-start.5 = (f32[4,64,128]{2,1,0:T(8,128)S(1)}, f32[4,64,128]{2,1,0:T(8,128)S(1)}, u32[]{:S(2)}, u32[]{:S(2)}) collective-permute-start(f32[4,64,128]{2,1,0:T(8,128)S(1)} %get-tuple-element.8), channel_id=1, source_target_pairs={{0,1},{1,0},{2,3},{3,2},{4,5},{5,4},{6,7},{7,6},{8,9},{9,8},{10,11... | collective-permute-start | bytes 393224 | tf_op jit(solution)/shard_map/ppermute | solution.py:143
  20.1 3.7 %collective-permute-start.7 = (f32[64,128]{1,0:T(8,128)S(1)}, f32[64,128]{1,0:T(8,128)S(1)}, u32[]{:S(2)}, u32[]{:S(2)}) collective-permute-start(f32[64,128]{1,0:T(8,128)S(1)} %get-tuple-element.9), channel_id=1, source_target_pairs={{0,3},{1,2},{2,1},{3,0},{4,5},{5,4},{6,13},{7,12},{8,7},{9,6},{10,... | collective-permute-start | bytes 98312 | tf_op jit(solution)/shard_map/ppermute | solution.py:192
  21.4 4.4 %collective-permute-start.9 = (f32[64,128]{1,0:T(8,128)S(1)}, f32[64,128]{1,0:T(8,128)S(1)}, u32[]{:S(2)}, u32[]{:S(2)}) collective-permute-start(f32[64,128]{1,0:T(8,128)S(1)} %get-tuple-element.10), channel_id=1, source_target_pairs={{0,5},{1,4},{2,13},{3,12},{4,3},{5,2},{6,1},{7,0},{8,15},{9,14},{1... | collective-permute-start | bytes 98312 | tf_op jit(solution)/shard_map/ppermute | solution.py:192
  21.7 4.0 %collective-permute-start.8 = (f32[64,128]{1,0:T(8,128)S(1)}, f32[64,128]{1,0:T(8,128)S(1)}, u32[]{:S(2)}, u32[]{:S(2)}) collective-permute-start(f32[64,128]{1,0:T(8,128)S(1)} %get-tuple-element.11), channel_id=1, source_target_pairs={{0,13},{1,12},{2,3},{3,2},{4,1},{5,0},{6,5},{7,4},{8,11},{9,10},{1... | collective-permute-start | bytes 98312 | tf_op jit(solution)/shard_map/ppermute | solution.py:192
  23.4 2.3 %collective-permute-start.6 = (f32[64,128]{1,0:T(8,128)S(1)}, f32[64,128]{1,0:T(8,128)S(1)}, u32[]{:S(2)}, u32[]{:S(2)}) collective-permute-start(f32[64,128]{1,0:T(8,128)S(1)} %get-tuple-element.12), channel_id=1, source_target_pairs={{0,1},{1,0},{2,5},{3,4},{4,13},{5,12},{6,3},{7,2},{8,9},{9,8},{10,... | collective-permute-start | bytes 98312 | tf_op jit(solution)/shard_map/ppermute | solution.py:192
